TPU v7x, 128 devices: a whole 4x4x4 slice. The times are simulated.
128 devices in a mesh: cfg: 2 (over x_lo), blk: 8 (over z, core), uly: 8 (over x_hi, y).
Axes of the slice: x: 4 (x_hi: 2, x_lo: 2; x = x_hi * 2 + x_lo), y: 4, z: 4, core: 2. Of those that a mesh axis runs over, the one named last changes fastest.
Arguments:
- new_queries: bfloat16 [8192, 6144], P(('cfg', 'blk', 'uly')), parts along dimension 0, may hold values from -15 to 15
- new_keys: bfloat16 [8192, 6144], P(('cfg', 'blk', 'uly')), parts along dimension 0, may hold values from -6 to 6
- new_values: bfloat16 [8192, 6144], P(('cfg', 'blk', 'uly')), parts along dimension 0, may hold values from -6 to 6
- context_keys: bfloat16 [16384, 6144], P(('cfg', 'blk'), 'uly'), parts along dimension 0, may hold values from -6 to 6
- context_values: bfloat16 [16384, 6144], P(('cfg', 'blk'), 'uly'), parts along dimension 0, may hold values from -6 to 6
- keep_flags: int32 [32, 96], replicated, may hold values from 0 to 1, as said below
Outputs:
- attended: bfloat16 [8192, 6144], P(('cfg', 'blk', 'uly')), parts along dimension 0
There are 2 independent parts, one for each index of `cfg`. A program takes and returns all parts, laid end to end along the dimension named above; an argument that names none is the same for every part. Nothing has to cross between parts.
Inputs may be any that keep to these rules, and one draw needn't show every extreme that they name: keep_flags[i, 0] and keep_flags[i, 64 + i] are 1 for every query block i; at least one query block keeps every key block.
All inputs are finite; a program needn't handle non-finite values.
Results may differ from a plain program's by a relative error of at most 0.017.
Values may be sent and summed in bfloat16 or wider, within the bound.
A program may use at most 128 MiB of HBM per device.

v0:
```python
import jax
import jax.numpy as jnp
from jax import lax
from jax.sharding import PartitionSpec as P

DH = 128
TILE = 128


masked_score = -1e30


def tile_numbers(row_count, context_rows, span_rows, cycle_size):
    row_index = jnp.arange(row_count, dtype=jnp.int32)
    local_rows = context_rows + span_rows
    holder = row_index // local_rows
    within = row_index % local_rows
    context_tile = (holder * context_rows + within) // TILE
    span_tile = (context_rows * cycle_size + holder * span_rows + within - context_rows) // TILE
    return jnp.where(within < context_rows, context_tile, span_tile)


def allowed_pairs(keep_rows, tile_ids):
    columns = jnp.take(keep_rows, tile_ids, axis=1)
    return jnp.repeat(columns, TILE, axis=0) > 0


def partial_softmax(queries, key_rows, value_rows, allowed):
    heads_here = queries.shape[1] // DH
    high_list = []
    total_list = []
    weighted_list = []
    for head in range(heads_here):
        query_head = queries[:, head * DH : (head + 1) * DH]
        key_head = key_rows[:, head * DH : (head + 1) * DH]
        value_head = value_rows[:, head * DH : (head + 1) * DH]
        scores = lax.dot_general(
            query_head, key_head, (((1,), (1,)), ((), ())), preferred_element_type=jnp.float32
        ) * DH ** (-0.5)
        scores = jnp.where(allowed, scores, masked_score)
        highest = jnp.max(scores, axis=1)
        weights = jnp.where(allowed, jnp.exp(scores - highest[:, None]), 0.0)
        high_list.append(highest)
        total_list.append(jnp.sum(weights, axis=1))
        weighted_list.append(
            jnp.dot(weights.astype(jnp.bfloat16), value_head, preferred_element_type=jnp.float32)
        )
    return (
        jnp.stack(high_list, axis=1),
        jnp.stack(total_list, axis=1),
        jnp.concatenate(weighted_list, axis=1),
    )


def join_states(earlier, later):
    highest = jnp.maximum(earlier[0], later[0])
    first_scale = jnp.exp(earlier[0] - highest)
    second_scale = jnp.exp(later[0] - highest)
    totals = earlier[1] * first_scale + later[1] * second_scale
    weighted = earlier[2] * jnp.repeat(first_scale, DH, axis=1) + later[2] * jnp.repeat(
        second_scale, DH, axis=1
    )
    return (highest, totals, weighted)


def shards(new_queries, new_keys, new_values, context_keys, context_values, keep_flags):
    span_queries, span_keys, span_values = (
        lax.all_to_all(new_queries, "uly", split_axis=1, concat_axis=0, tiled=True),
        lax.all_to_all(new_keys, "uly", split_axis=1, concat_axis=0, tiled=True),
        lax.all_to_all(new_values, "uly", split_axis=1, concat_axis=0, tiled=True),
    )
    span_rows = span_queries.shape[0]
    head_width = span_queries.shape[1]
    heads_here = head_width // DH
    context_rows = context_keys.shape[0]
    cycle_size = lax.axis_size("blk")
    cycle_index = lax.axis_index("blk")
    query_tiles = span_rows // TILE
    local_keys = jnp.concatenate([context_keys, span_keys], axis=0)
    local_values = jnp.concatenate([context_values, span_values], axis=0)
    keep_rows = lax.dynamic_slice_in_dim(keep_flags, cycle_index * query_tiles, query_tiles, 0)
    start_state = (
        jnp.full((span_rows, heads_here), masked_score, jnp.float32),
        jnp.zeros((span_rows, heads_here), jnp.float32),
        jnp.zeros((span_rows, head_width), jnp.float32),
    )
    carried_state = start_state
    key_piece = lax.all_gather(local_keys, "blk", axis=0, tiled=True)
    value_piece = lax.all_gather(local_values, "blk", axis=0, tiled=True)
    row_count = key_piece.shape[0]
    allowed = allowed_pairs(keep_rows, tile_numbers(row_count, context_rows, span_rows, cycle_size))
    block_width = 512
    blocks = row_count // block_width

    def advance(running, block_number):
        start = block_number * block_width
        key_block = lax.dynamic_slice_in_dim(key_piece, start, block_width, 0)
        value_block = lax.dynamic_slice_in_dim(value_piece, start, block_width, 0)
        mask_block = lax.dynamic_slice_in_dim(allowed, start, block_width, 1)
        found = partial_softmax(span_queries, key_block, value_block, mask_block)
        return (join_states(running, found), None)

    carried_state, unused = lax.scan(advance, carried_state, jnp.arange(blocks, dtype=jnp.int32))
    highest, totals, weighted = carried_state
    attended = (weighted / jnp.repeat(totals, DH, axis=1)).astype(jnp.bfloat16)
    return lax.all_to_all(attended, "uly", split_axis=0, concat_axis=1, tiled=True)


def solution(mesh):
    in_specs = (
        P(("cfg", "blk", "uly"), None),
        P(("cfg", "blk", "uly"), None),
        P(("cfg", "blk", "uly"), None),
        P(("cfg", "blk"), "uly"),
        P(("cfg", "blk"), "uly"),
        P(),
    )
    out_specs = P(("cfg", "blk", "uly"), None)
    return jax.shard_map(shards, mesh=mesh, in_specs=in_specs, out_specs=out_specs, check_vma=False)
```

profile of v0, /device:TPU:24, one launch (start us, length us, event | category | flops | bytes accessed | tf_op | source)
XLA Modules:
  0.0 832.6 jit_solution(14795615542286856412)
XLA Ops:
  7.8 19.0 %all_to_all.76 = bf16[64,8,768]{2,0,1:T(8,128)(2,1)S(1)} all-to-all(bf16[64,8,768]{2,0,1:T(8,128)(2,1)S(1)} %bitcast.119), channel_id=1, replica_groups=mesh['cfg'=2,'blk'=8,'uly'=8] {'uly'}, dimensions={1} | all-to-all | bytes 1572864 | tf_op jit(solution)/shard_map/all_to_all | solution.py:70
  26.8 2.9 pad_maximum_fusion.1
  29.9 15.9 %all_to_all.77 = bf16[64,8,768]{2,0,1:T(8,128)(2,1)S(1)} all-to-all(bf16[64,8,768]{2,0,1:T(8,128)(2,1)S(1)} %bitcast.120), channel_id=1, replica_groups=mesh['cfg'=2,'blk'=8,'uly'=8] {'uly'}, dimensions={1} | all-to-all | bytes 1572864 | tf_op jit(solution)/shard_map/all_to_all | solution.py:69
  48.3 6.5 all-to-all-start.1
  55.7 41.0 %gather_fusion = s32[12288,4]{1,0:T(8,128)} fusion(s32[4,96]{0,1:T(8,128)S(1)} %copy.24, s32[12288]{0:T(1024)S(1)} %broadcast_clamp_fusion), kind=kCustom, calls=%fused_computation | custom fusion | bytes 442368 | tf_op jit(solution)/shard_map/jit(_take)/gather | solution.py:24
  96.8 9.1 %fusion.70 = pred[4,12288]{0,1:T(8,128)(4,1)S(1)} fusion(s32[12288,4]{1,0:T(8,128)} %gather_fusion, pred[12288]{0:T(1024)(128)(4,1)S(1)} %compare_and_fusion), kind=kLoop, calls=%fused_computation.92 | loop fusion | flops 98304 | bytes 258048 | tf_op jit(solution)/shard_map/gt | solution.py:25
  106.0 16.6 %broadcast_in_dim.59 = pred[4,128,12288]{1,0,2:T(4,128)(4,1)S(1)} broadcast(pred[4,12288]{0,1:T(8,128)(4,1)S(1)} %fusion.70), dimensions={0,2} | broadcast | bytes 6340608 | tf_op jit(solution)/shard_map/broadcast_in_dim | solution.py:25
  122.6 4.0 copy.34
  126.6 4.5 copy.55
  131.1 89.3 %all-gather.3.cloned.1.call-done = bf16[12288,768]{1,0:T(8,128)(2,1)} async-done(((bf16[1536,768]{1,0:T(8,128)(2,1)}), bf16[12288,768]{1,0:T(8,128)(2,1)}) %all-gather.3.cloned.1.call-update) | async-done | bytes 18874384 | tf_op jit(solution)/shard_map/all_gather | solution.py:88
  220.4 583.3 %while.15 = (s32[]{:T(128)}, f32[512,6]{0,1:T(8,128)S(1)}, f32[512,6]{0,1:T(8,128)S(1)}, f32[512,768]{0,1:T(8,128)}, s32[24]{0:T(128)S(1)}, /*index=5*/pred[512,...) while((s32[]{:T(128)}, f32[512,6]{0,1:T(8,128)S(1)}, ...), condition=%wide.region_13.14_spmd.clone, body=%wide.region_0.13_spmd.clone.sunk | while | flops 821053440 | bytes 56337852 | solution.py:103
  231.4 2.1 fusion.133
  255.7 2.1 fusion.133
  280.0 2.1 fusion.133
  304.3 2.1 fusion.133
  328.6 2.1 fusion.133
  352.9 2.1 fusion.133
  377.2 2.1 fusion.133
  401.5 2.1 fusion.133
  425.8 2.1 fusion.133
  450.1 2.1 fusion.133
  474.4 2.1 fusion.133
  498.7 2.1 fusion.133
  523.0 2.1 fusion.133
  547.3 2.1 fusion.133
  571.6 2.1 fusion.133
  596.0 2.1 fusion.133
  620.3 2.1 fusion.133
  644.6 2.1 fusion.133
  741.8 2.1 fusion.133
  766.1 2.1 fusion.133
  805.5 19.3 %all_to_all.78 = bf16[8,64,768]{2,1,0:T(8,128)(2,1)S(1)} all-to-all(bf16[8,64,768]{2,1,0:T(8,128)(2,1)S(1)} %bitcast.117), channel_id=1, replica_groups=mesh['cfg'=2,'blk'=8,'uly'=8] {'uly'}, dimensions={0} | all-to-all | bytes 1572864 | tf_op jit(solution)/shard_map/all_to_all | solution.py:106
  (684 shorter events, 529.7 us)
Async XLA Ops:
  6.5 48.3 %copy-start = (s32[32,96]{1,0:T(8,128)S(1)}, s32[32,96]{1,0:T(8,128)}, u32[]{:S(2)}) copy-start(s32[32,96]{1,0:T(8,128)} %param.13) | copy-start | bytes 36868
  6.5 23.3 %copy-start.8 = (bf16[64,6144]{1,0:T(8,128)(2,1)S(1)}, bf16[64,6144]{1,0:T(8,128)(2,1)}, u32[]{:S(2)}) copy-start(bf16[64,6144]{1,0:T(8,128)(2,1)} %param.9) | copy-start | bytes 2359300
  6.5 124.6 %all-gather.5.cloned.1.call-start = ((), (), s32[]{:S(2)}) async-start(), calls=%async_computation.5 | async-start | bytes 21233664 | tf_op jit(solution)/shard_map/all_gather | solution.py:89
  7.8 38.0 %copy-start.7 = (bf16[1024,768]{1,0:T(8,128)(2,1)S(1)}, bf16[1024,768]{1,0:T(8,128)(2,1)}, u32[]{:S(2)}) copy-start(bf16[1024,768]{1,0:T(8,128)(2,1)} %param.11) | copy-start | bytes 4718596
  29.8 17.6 %copy-start.9 = (bf16[64,6144]{1,0:T(8,128)(2,1)S(1)}, bf16[64,6144]{1,0:T(8,128)(2,1)}, u32[]{:S(2)}) copy-start(bf16[64,6144]{1,0:T(8,128)(2,1)} %param.8) | copy-start | bytes 2359300
  29.8 190.6 %all-gather.3.cloned.1.call-start = ((), (), s32[]{:S(2)}) async-start(), calls=%async_computation.4 | async-start | bytes 21233664 | tf_op jit(solution)/shard_map/all_gather | solution.py:88
  48.3 82.8 %all-to-all-start.1 = ((bf16[64,8,768]{2,0,1:T(8,128)(2,1)}), bf16[64,8,768]{2,0,1:T(8,128)(2,1)}, u32[]{:S(2)}, u32[]{:S(2)}) async-start(bf16[64,8,768]{2,0,1:T(8,128)(2,1)} %bitcast.81), calls=%async_computation.1 | async-start | bytes 1572864 | tf_op jit(solution)/shard_map/all_to_all | solution.py:68
  233.6 9.3 %copy-start.5 = (f32[512,768]{0,1:T(8,128)S(1)}, f32[512,768]{0,1:T(8,128)}, u32[]{:S(2)}) copy-start(f32[512,768]{0,1:T(8,128)} %get-tuple-element.245) | copy-start | bytes 4718596 | tf_op jit(solution)/shard_map/while
  257.9 9.3 %copy-start.5 = (f32[512,768]{0,1:T(8,128)S(1)}, f32[512,768]{0,1:T(8,128)}, u32[]{:S(2)}) copy-start(f32[512,768]{0,1:T(8,128)} %get-tuple-element.245) | copy-start | bytes 4718596 | tf_op jit(solution)/shard_map/while
  282.2 9.3 %copy-start.5 = (f32[512,768]{0,1:T(8,128)S(1)}, f32[512,768]{0,1:T(8,128)}, u32[]{:S(2)}) copy-start(f32[512,768]{0,1:T(8,128)} %get-tuple-element.245) | copy-start | bytes 4718596 | tf_op jit(solution)/shard_map/while
  306.5 9.3 %copy-start.5 = (f32[512,768]{0,1:T(8,128)S(1)}, f32[512,768]{0,1:T(8,128)}, u32[]{:S(2)}) copy-start(f32[512,768]{0,1:T(8,128)} %get-tuple-element.245) | copy-start | bytes 4718596 | tf_op jit(solution)/shard_map/while
  330.8 9.3 %copy-start.5 = (f32[512,768]{0,1:T(8,128)S(1)}, f32[512,768]{0,1:T(8,128)}, u32[]{:S(2)}) copy-start(f32[512,768]{0,1:T(8,128)} %get-tuple-element.245) | copy-start | bytes 4718596 | tf_op jit(solution)/shard_map/while
  355.1 9.3 %copy-start.5 = (f32[512,768]{0,1:T(8,128)S(1)}, f32[512,768]{0,1:T(8,128)}, u32[]{:S(2)}) copy-start(f32[512,768]{0,1:T(8,128)} %get-tuple-element.245) | copy-start | bytes 4718596 | tf_op jit(solution)/shard_map/while
  379.4 9.3 %copy-start.5 = (f32[512,768]{0,1:T(8,128)S(1)}, f32[512,768]{0,1:T(8,128)}, u32[]{:S(2)}) copy-start(f32[512,768]{0,1:T(8,128)} %get-tuple-element.245) | copy-start | bytes 4718596 | tf_op jit(solution)/shard_map/while
  403.7 9.3 %copy-start.5 = (f32[512,768]{0,1:T(8,128)S(1)}, f32[512,768]{0,1:T(8,128)}, u32[]{:S(2)}) copy-start(f32[512,768]{0,1:T(8,128)} %get-tuple-element.245) | copy-start | bytes 4718596 | tf_op jit(solution)/shard_map/while
  428.0 9.3 %copy-start.5 = (f32[512,768]{0,1:T(8,128)S(1)}, f32[512,768]{0,1:T(8,128)}, u32[]{:S(2)}) copy-start(f32[512,768]{0,1:T(8,128)} %get-tuple-element.245) | copy-start | bytes 4718596 | tf_op jit(solution)/shard_map/while
  452.3 9.3 %copy-start.5 = (f32[512,768]{0,1:T(8,128)S(1)}, f32[512,768]{0,1:T(8,128)}, u32[]{:S(2)}) copy-start(f32[512,768]{0,1:T(8,128)} %get-tuple-element.245) | copy-start | bytes 4718596 | tf_op jit(solution)/shard_map/while
  476.6 9.3 %copy-start.5 = (f32[512,768]{0,1:T(8,128)S(1)}, f32[512,768]{0,1:T(8,128)}, u32[]{:S(2)}) copy-start(f32[512,768]{0,1:T(8,128)} %get-tuple-element.245) | copy-start | bytes 4718596 | tf_op jit(solution)/shard_map/while
  500.9 9.3 %copy-start.5 = (f32[512,768]{0,1:T(8,128)S(1)}, f32[512,768]{0,1:T(8,128)}, u32[]{:S(2)}) copy-start(f32[512,768]{0,1:T(8,128)} %get-tuple-element.245) | copy-start | bytes 4718596 | tf_op jit(solution)/shard_map/while
  525.2 9.3 %copy-start.5 = (f32[512,768]{0,1:T(8,128)S(1)}, f32[512,768]{0,1:T(8,128)}, u32[]{:S(2)}) copy-start(f32[512,768]{0,1:T(8,128)} %get-tuple-element.245) | copy-start | bytes 4718596 | tf_op jit(solution)/shard_map/while
  549.5 9.3 %copy-start.5 = (f32[512,768]{0,1:T(8,128)S(1)}, f32[512,768]{0,1:T(8,128)}, u32[]{:S(2)}) copy-start(f32[512,768]{0,1:T(8,128)} %get-tuple-element.245) | copy-start | bytes 4718596 | tf_op jit(solution)/shard_map/while
  573.8 9.3 %copy-start.5 = (f32[512,768]{0,1:T(8,128)S(1)}, f32[512,768]{0,1:T(8,128)}, u32[]{:S(2)}) copy-start(f32[512,768]{0,1:T(8,128)} %get-tuple-element.245) | copy-start | bytes 4718596 | tf_op jit(solution)/shard_map/while
  598.1 9.3 %copy-start.5 = (f32[512,768]{0,1:T(8,128)S(1)}, f32[512,768]{0,1:T(8,128)}, u32[]{:S(2)}) copy-start(f32[512,768]{0,1:T(8,128)} %get-tuple-element.245) | copy-start | bytes 4718596 | tf_op jit(solution)/shard_map/while
  622.4 9.3 %copy-start.5 = (f32[512,768]{0,1:T(8,128)S(1)}, f32[512,768]{0,1:T(8,128)}, u32[]{:S(2)}) copy-start(f32[512,768]{0,1:T(8,128)} %get-tuple-element.245) | copy-start | bytes 4718596 | tf_op jit(solution)/shard_map/while
  646.7 9.3 %copy-start.5 = (f32[512,768]{0,1:T(8,128)S(1)}, f32[512,768]{0,1:T(8,128)}, u32[]{:S(2)}) copy-start(f32[512,768]{0,1:T(8,128)} %get-tuple-element.245) | copy-start | bytes 4718596 | tf_op jit(solution)/shard_map/while
  671.0 9.3 %copy-start.5 = (f32[512,768]{0,1:T(8,128)S(1)}, f32[512,768]{0,1:T(8,128)}, u32[]{:S(2)}) copy-start(f32[512,768]{0,1:T(8,128)} %get-tuple-element.245) | copy-start | bytes 4718596 | tf_op jit(solution)/shard_map/while
  695.3 9.3 %copy-start.5 = (f32[512,768]{0,1:T(8,128)S(1)}, f32[512,768]{0,1:T(8,128)}, u32[]{:S(2)}) copy-start(f32[512,768]{0,1:T(8,128)} %get-tuple-element.245) | copy-start | bytes 4718596 | tf_op jit(solution)/shard_map/while
  719.6 9.3 %copy-start.5 = (f32[512,768]{0,1:T(8,128)S(1)}, f32[512,768]{0,1:T(8,128)}, u32[]{:S(2)}) copy-start(f32[512,768]{0,1:T(8,128)} %get-tuple-element.245) | copy-start | bytes 4718596 | tf_op jit(solution)/shard_map/while
  743.9 9.3 %copy-start.5 = (f32[512,768]{0,1:T(8,128)S(1)}, f32[512,768]{0,1:T(8,128)}, u32[]{:S(2)}) copy-start(f32[512,768]{0,1:T(8,128)} %get-tuple-element.245) | copy-start | bytes 4718596 | tf_op jit(solution)/shard_map/while
  768.2 9.3 %copy-start.5 = (f32[512,768]{0,1:T(8,128)S(1)}, f32[512,768]{0,1:T(8,128)}, u32[]{:S(2)}) copy-start(f32[512,768]{0,1:T(8,128)} %get-tuple-element.245) | copy-start | bytes 4718596 | tf_op jit(solution)/shard_map/while
  792.5 9.3 %copy-start.5 = (f32[512,768]{0,1:T(8,128)S(1)}, f32[512,768]{0,1:T(8,128)}, u32[]{:S(2)}) copy-start(f32[512,768]{0,1:T(8,128)} %get-tuple-element.245) | copy-start | bytes 4718596 | tf_op jit(solution)/shard_map/while
  803.7 22.1 %copy-start.1 = (s32[32,96]{1,0:T(8,128)S(1)}, s32[32,96]{1,0:T(8,128)}, u32[]{:S(2)}) copy-start(s32[32,96]{1,0:T(8,128)} %param.13) | copy-start | bytes 36868
  (96 other events, 390.5 us)
Sparse Core Ops, SparseCore 0:
  29.9 94.1 all-gather.4
  125.8 94.5 all-gather.2
where the time goes:
time: 844 us; the launch traced here: 833 us
  matrix products  455 us (54%)
  local copies, waits for them, and re-layouts  113 us (13%)
  waiting for transfers between devices  89.3 us (11%)
  other arithmetic  81.4 us (10%)
  blocking collectives  54.2 us (6%)
  loops' own time  19.6 us (2%)
  between operations  13.5 us (2%)
    dot_general x144, matrix products, partial_softmax(): lax.dot_general(query_head, key_head, (((1,), (1,)), ((), ())), preferred...  233 us
    dot_general x144, matrix products, partial_softmax(): jnp.dot(weights.astype(jnp.bfloat16), value_head, preferred_element_type=...  222 us
    all_gather x1, waiting for transfers between devices, shards(): key_piece = lax.all_gather(local_keys, 'blk', axis=0, tiled=True)  89.3 us
    reduce_sum x24, other arithmetic, partial_softmax(): total_list.append(jnp.sum(weights, axis=1))  50 us
    gather x1, local copies, waits for them, and re-layouts, allowed_pairs(): columns = jnp.take(keep_rows, tile_ids, axis=1)  41 us
    while x240, local copies, waits for them, and re-layouts  28 us
    another operation x1, loops' own time, shards(): lax.scan(advance, carried_state, jnp.arange(blocks, dtype=jnp.int32))  19.6 us
    all_to_all x1, blocking collectives, shards(): lax.all_to_all(attended, 'uly', split_axis=0, concat_axis=1, tiled=True)  19.3 us
  transfers between devices with their start and end apart: 3, of which 1 were waited for; matrix products, arithmetic and copies ran while one was open for 9% of the time, Pallas kernels for 0%

commit v1 on v0

v1 whole, which is shorter than its diff:
```python
import functools

import jax
import jax.numpy as jnp
from jax import lax
from jax.experimental import pallas as pl
from jax.experimental.pallas import tpu as pltpu
from jax.sharding import PartitionSpec as P

DH = 128
TILE = 128
HEADS = 6
ROWS = 144
LOW = -1e30
LOG2 = 1.4426950408889634 * DH ** (-0.5)


def attend_kernel(order_ref, count_ref, q_ref, k_ref, v_ref, o_ref, lse_ref, vt, acc, top):
    step = pl.program_id(0)
    tiles = vt.shape[0]

    @pl.when(step == 0)
    def _():
        def turn(t, carry):
            rows = pl.ds(pl.multiple_of(t * TILE, TILE), TILE)
            for h in range(HEADS):
                vt[t, h * ROWS : h * ROWS + DH, :] = v_ref[rows, h * DH : (h + 1) * DH].T
                vt[t, h * ROWS + DH : (h + 1) * ROWS, :] = jnp.ones((ROWS - DH, TILE), jnp.bfloat16)
            return carry

        lax.fori_loop(0, tiles, turn, 0)

    acc[...] = jnp.zeros_like(acc)
    top[...] = jnp.full_like(top, LOW)
    count = count_ref[step]

    def visit(picked):
        for h in range(HEADS):
            cols = slice(h * DH, (h + 1) * DH)
            q = q_ref[:, cols]
            s = [
                lax.dot_general(
                    k_ref[pl.ds(pl.multiple_of(t * TILE, TILE), TILE), cols],
                    q,
                    (((1,), (1,)), ((), ())),
                    preferred_element_type=jnp.float32,
                )
                for t in picked
            ]
            s = s[0] if len(s) == 1 else jnp.concatenate(s, axis=0)
            old = top[h : h + 1, :]
            new = jnp.maximum(old, jnp.max(s, axis=0, keepdims=True))
            top[h : h + 1, :] = new
            p = jnp.exp2((s - new) * LOG2).astype(jnp.bfloat16)
            scale = jnp.exp2((old - new) * LOG2)
            vs = [vt[t, h * ROWS : (h + 1) * ROWS, :] for t in picked]
            vs = vs[0] if len(vs) == 1 else jnp.concatenate(vs, axis=1)
            acc[h] = acc[h] * scale + jnp.dot(vs, p, preferred_element_type=jnp.float32)

    def pair(j, carry):
        visit([order_ref[step, 2 * j], order_ref[step, 2 * j + 1]])
        return carry

    lax.fori_loop(0, count // 2, pair, 0)

    @pl.when(count % 2 == 1)
    def _():
        visit([order_ref[step, count - 1]])

    for h in range(HEADS):
        total = acc[h, DH : DH + 1, :]
        any_key = total > 0
        safe = jnp.where(any_key, total, 1.0)
        o_ref[0, h * DH : (h + 1) * DH, :] = (acc[h, :DH, :] * (1.0 / safe)).astype(jnp.bfloat16)
        lse_ref[0, h : h + 1, :] = jnp.where(any_key, top[h : h + 1, :] * LOG2 + jnp.log2(safe), LOW)
    lse_ref[0, HEADS:, :] = jnp.full((8 - HEADS, TILE), LOW, jnp.float32)


def attend(order, counts, queries, keys, values):
    steps = queries.shape[0] // TILE
    tiles = keys.shape[0] // TILE
    width = queries.shape[1]
    whole = pl.BlockSpec(keys.shape, lambda i, *_: (0, 0))
    return pl.pallas_call(
        attend_kernel,
        out_shape=(
            jax.ShapeDtypeStruct((steps, width, TILE), jnp.bfloat16),
            jax.ShapeDtypeStruct((steps, 8, TILE), jnp.float32),
        ),
        grid_spec=pltpu.PrefetchScalarGridSpec(
            num_scalar_prefetch=2,
            grid=(steps,),
            in_specs=[pl.BlockSpec((TILE, width), lambda i, *_: (i, 0)), whole, whole],
            out_specs=(
                pl.BlockSpec((1, width, TILE), lambda i, *_: (i, 0, 0)),
                pl.BlockSpec((1, 8, TILE), lambda i, *_: (i, 0, 0)),
            ),
            scratch_shapes=[
                pltpu.VMEM((tiles, HEADS * ROWS, TILE), jnp.bfloat16),
                pltpu.VMEM((HEADS, ROWS, TILE), jnp.float32),
                pltpu.VMEM((8, TILE), jnp.float32),
            ],
        ),
        compiler_params=pltpu.CompilerParams(vmem_limit_bytes=40 * 1024 * 1024),
        cost_estimate=pl.CostEstimate(flops=6 * 10**9, bytes_accessed=18 * 10**6, transcendentals=12 * 10**6),
    )(order, counts, queries, keys, values)


def kept_tiles(keep_flags, ctx_tiles, span_tiles, blk, cycle):
    ctx = lax.dynamic_slice_in_dim(keep_flags, blk * ctx_tiles, ctx_tiles, 1)
    span = lax.dynamic_slice_in_dim(keep_flags, cycle * ctx_tiles + blk * span_tiles, span_tiles, 1)
    mine = (jnp.concatenate([ctx, span], axis=1) > 0).astype(jnp.int32)
    n = mine.shape[1]
    place = jnp.cumsum(mine, axis=1) - 1
    slot = jnp.arange(n, dtype=jnp.int32)
    hit = (place[:, :, None] == slot[None, None, :]) & (mine[:, :, None] > 0)
    order = jnp.sum(jnp.where(hit, slot[None, :, None], 0), axis=1)
    return order, jnp.sum(mine, axis=1)


def shards(new_queries, new_keys, new_values, context_keys, context_values, keep_flags):
    span_queries = lax.all_to_all(new_queries, "uly", split_axis=1, concat_axis=0, tiled=True)
    queries = lax.all_gather(span_queries, "blk", axis=0, tiled=True)
    span_keys = lax.all_to_all(new_keys, "uly", split_axis=1, concat_axis=0, tiled=True)
    span_values = lax.all_to_all(new_values, "uly", split_axis=1, concat_axis=0, tiled=True)
    keys = jnp.concatenate([context_keys, span_keys], axis=0)
    values = jnp.concatenate([context_values, span_values], axis=0)
    cycle = lax.axis_size("blk")
    blk = lax.axis_index("blk")
    order, counts = kept_tiles(
        keep_flags, context_keys.shape[0] // TILE, span_keys.shape[0] // TILE, blk, cycle
    )
    part, lse = attend(order, counts, queries, keys, values)
    lse = lse[:, :HEADS, :]
    best = lax.pmax(lse, "blk")
    weight = jnp.exp2(lse - best)
    steps = part.shape[0]
    scaled = part.reshape(steps, HEADS, DH, TILE).astype(jnp.float32) * weight[:, :, None, :]
    weighted = lax.psum_scatter(scaled, "blk", scatter_dimension=0, tiled=True)
    totals = lax.psum_scatter(weight, "blk", scatter_dimension=0, tiled=True)
    mine = (weighted / totals[:, :, None, :]).astype(jnp.bfloat16)
    attended = mine.transpose(0, 3, 1, 2).reshape(-1, HEADS * DH)
    return lax.all_to_all(attended, "uly", split_axis=0, concat_axis=1, tiled=True)


def solution(mesh):
    in_specs = (
        P(("cfg", "blk", "uly"), None),
        P(("cfg", "blk", "uly"), None),
        P(("cfg", "blk", "uly"), None),
        P(("cfg", "blk"), "uly"),
        P(("cfg", "blk"), "uly"),
        P(),
    )
    out_specs = P(("cfg", "blk", "uly"), None)
    return jax.shard_map(shards, mesh=mesh, in_specs=in_specs, out_specs=out_specs, check_vma=False)
```

time: 844 us -> 390 us (0.46)
  matrix products: 455 us -> 0 us
  waiting for transfers between devices: 89.3 us -> 186 us
  Pallas kernels: 0 us -> 91.7 us
  local copies, waits for them, and re-layouts: 113 us -> 22.9 us
  other arithmetic: 81.4 us -> 23.7 us
  loops' own time: 19.6 us -> 0 us
  blocking collectives: 54.2 us -> 37.2 us
    dot_general x288 -> x0, matrix products: 455 us -> none  [the longest x144 233 us: partial_softmax(): lax.dot_general(query_head, key_head, (((1,), (1,)), ((), ())), preferred...]
    reduce_scatter x0 -> x2, waiting for transfers between devices: none -> 107 us  [the longest x1 92.1 us: shards(): weighted = lax.psum_scatter(scaled, 'blk', scatter_dimension=0, tiled=True)]
    pallas_call x0 -> x1, Pallas kernels: none -> 91.7 us  [attend(): pl.pallas_call(attend_kernel, out_shape=(jax.ShapeDtypeStruct((steps, wid...]
    all_gather x2 -> x1, waiting for transfers between devices: 89.3 us -> 4.32 us  [shards(): queries = lax.all_gather(span_queries, 'blk', axis=0, tiled=True)]
    pmax x0 -> x1, waiting for transfers between devices: none -> 57.2 us  [shards(): best = lax.pmax(lse, 'blk')]
    reduce_sum x24 -> x2, other arithmetic: 50 us -> 0.22 us  [the longest x1 0.18 us: kept_tiles(): return (order, jnp.sum(mine, axis=1))]
    gather x1 -> x0, local copies, waits for them, and re-layouts: 41 us -> none  [allowed_pairs(): columns = jnp.take(keep_rows, tile_ids, axis=1)]
    while x240 -> x0, local copies, waits for them, and re-layouts: 28 us -> none
  transfers between devices with their start and end apart: 3 -> 6, of which waited for: 1 -> 6; matrix products, arithmetic and copies ran while one was open for 9% -> 9% of each run, Pallas kernels for 0% -> 0%
where the time goes in v1:
time: 390 us; the launch traced here: 387 us
  waiting for transfers between devices  186 us (48%)
  Pallas kernels  91.7 us (24%)
  blocking collectives  37.2 us (10%)
  other arithmetic  23.7 us (6%)
  local copies, waits for them, and re-layouts  22.9 us (6%)
  between operations  13.2 us (3%)
  starting transfers between devices  12 us (3%)
    reduce_scatter x1, waiting for transfers between devices, shards(): weighted = lax.psum_scatter(scaled, 'blk', scatter_dimension=0, tiled=True)  92.1 us
    pallas_call x1, Pallas kernels, attend(): pl.pallas_call(attend_kernel, out_shape=(jax.ShapeDtypeStruct((steps, wid...  91.7 us
    pmax x1, waiting for transfers between devices, shards(): best = lax.pmax(lse, 'blk')  57.2 us
    all_to_all x1, blocking collectives, shards(): lax.all_to_all(new_queries, 'uly', split_axis=1, concat_axis=0, tiled=True)  19 us
    all_to_all x1, blocking collectives, shards(): lax.all_to_all(attended, 'uly', split_axis=0, concat_axis=1, tiled=True)  18.2 us
    mul x1, other arithmetic, shards(): part.reshape(steps, HEADS, DH, TILE).astype(jnp.float32)  15.3 us
    reduce_scatter x1, waiting for transfers between devices, shards(): totals = lax.psum_scatter(weight, 'blk', scatter_dimension=0, tiled=True)  14.8 us
    convert_element_type x1, local copies, waits for them, and re-layouts, shards(): part.reshape(steps, HEADS, DH, TILE).astype(jnp.float32)  11.6 us
  transfers between devices with their start and end apart: 6, of which 6 were waited for; matrix products, arithmetic and copies ran while one was open for 9% of the time, Pallas kernels for 0%

profile of v1, /device:TPU:24, one launch (start us, length us, event | category | flops | bytes accessed | tf_op | source)
XLA Modules:
  0.0 386.6 jit_solution(6737558391093178031)
XLA Ops:
  6.5 1.3 copy.42
  7.8 19.0 %all_to_all.76 = bf16[64,8,768]{2,0,1:T(8,128)(2,1)} all-to-all(bf16[64,8,768]{2,0,1:T(8,128)(2,1)S(1)} %bitcast.33), channel_id=1, replica_groups=mesh['cfg'=2,'blk'=8,'uly'=8] {'uly'}, dimensions={1} | all-to-all | bytes 1572864 | tf_op jit(solution)/shard_map/all_to_all | solution.py:122
  26.8 0.9 copy.41
  27.8 5.9 %all-to-all-start.1 = ((bf16[64,8,768]{2,0,1:T(8,128)(2,1)}), bf16[64,8,768]{2,0,1:T(8,128)(2,1)S(1)}, u32[]{:S(2)}, u32[]{:S(2)}) async-start(bf16[64,8,768]{2,0,1:T(8,128)(2,1)} %bitcast.26), calls=%async_computation.1 | async-start | bytes 1572864 | tf_op jit(solution)/shard_map/all_to_all | solution.py:124
  33.6 0.1 constant_dynamic-slice_fusion
  33.8 0.2 fusion.3
  34.0 0.2 reduce_window_sum.11
  34.1 1.0 copy.40
  35.1 8.7 %all-to-all-done.1 = bf16[64,8,768]{2,0,1:T(8,128)(2,1)S(1)} async-done(((bf16[64,8,768]{2,0,1:T(8,128)(2,1)}), bf16[64,8,768]{2,0,1:T(8,128)(2,1)S(1)}, u32[]{:S(2)}, u32[]{:S(2)}) %all-to-all-start.1) | async-done | bytes 786464 | tf_op jit(solution)/shard_map/all_to_all | solution.py:124
  43.8 6.0 %all-to-all-start.2 = ((bf16[64,8,768]{2,0,1:T(8,128)(2,1)}), bf16[64,8,768]{2,0,1:T(8,128)(2,1)}, u32[]{:S(2)}, u32[]{:S(2)}) async-start(bf16[64,8,768]{2,0,1:T(8,128)(2,1)} %bitcast.25), calls=%async_computation.2 | async-start | bytes 1572864 | tf_op jit(solution)/shard_map/all_to_all | solution.py:125
  49.8 0.1 copy.23
  49.9 0.1 copy.24
  50.1 0.1 copy.28.order_ref
  50.2 1.7 pad_maximum_fusion.k_ref
  51.8 8.8 %all-to-all-done.2 = bf16[64,8,768]{2,0,1:T(8,128)(2,1)} async-done(((bf16[64,8,768]{2,0,1:T(8,128)(2,1)}), bf16[64,8,768]{2,0,1:T(8,128)(2,1)}, u32[]{:S(2)}, u32[]{:S(2)}) %all-to-all-start.2) | async-done | bytes 786464 | tf_op jit(solution)/shard_map/all_to_all | solution.py:125
  60.6 3.3 pad_maximum_fusion.1.v_ref
  63.9 4.3 %all-gather.2.cloned.1.call-done.q_ref = bf16[4096,768]{1,0:T(8,128)(2,1)} async-done(((bf16[512,768]{1,0:T(8,128)(2,1)}), bf16[4096,768]{1,0:T(8,128)(2,1)}) %all-gather.2.cloned.1.call-update) | async-done | bytes 6291472 | tf_op jit(solution)/shard_map/all_gather | solution.py:123
  68.3 1.7 copy-done.3
  69.9 91.7 %shard_map.64 = (bf16[32,768,128]{2,1,0:T(8,128)(2,1)S(1)}, f32[32,8,128]{2,1,0:T(8,128)}) custom-call(s32[32,12]{1,0:T(8,128)S(1)} %copy.28.order_ref, s32[32]{0:T(128)S(1)} %get-tuple-element.9.count_ref, bf16[4096,768]{1,0:T(8,128)(2,1)} %all-gather.2.cloned.1.call-done.q_ref, bf16[1536,768]{1,0:T(8,128)(2,1)S(1)} %pad_maximum_fusion.k_ref, ...), custom_call_target="tpu_custom_call" | custom-call | flops 6000000000 | bytes 18000000 | tf_op jit(solution)/shard_map/pallas_call | solution.py:84
  161.6 2.6 copy-done.2
  164.4 11.6 %copy.30 = f32[32,6,128,128]{2,1,3,0:T(8,128)} copy(bf16[32,6,128,128]{3,2,1,0:T(8,128)(2,1)} %bitcast.29) | data formatting | bytes 18874368 | tf_op jit(solution)/shard_map/convert_element_type | solution.py:138
  176.0 57.2 %all-reduce.2.cloned.1.call-done = f32[32,6,128]{2,1,0:T(8,128)} async-done(((f32[32,6,128]{2,1,0:T(8,128)}), f32[32,6,128]{2,1,0:T(8,128)}) %all-reduce.2.cloned.1.call-update) | async-done | bytes 98320 | tf_op jit(solution)/shard_map/pmax | solution.py:135
  233.2 1.0 multiply_exponential_fusion
  234.2 0.6 copy.29
  234.9 15.3 %broadcast_multiply_fusion = f32[32,6,128,128]{2,1,3,0:T(8,128)} fusion(f32[32,6,128,128]{2,1,3,0:T(8,128)} %copy.30, f32[32,6,128]{1,2,0:T(8,128)S(1)} %copy.29), kind=kLoop, calls=%fused_computation | loop fusion | flops 3145728 | bytes 25264128 | tf_op jit(solution)/shard_map/mul | solution.py:138
  250.3 14.8 %reduce-scatter.5.cloned.1.call-done = f32[4,6,128]{2,1,0:T(8,128)} async-done(((f32[32,6,128]{2,1,0:T(8,128)}), f32[4,6,128]{2,1,0:T(8,128)}) %reduce-scatter.5.cloned.1.call-update) | async-done | bytes 12304 | tf_op jit(solution)/shard_map/reduce_scatter | solution.py:140
  265.1 0.9 copy.31
  265.9 92.1 %reduce-scatter.3.cloned.1.call-done = f32[4,6,128,128]{2,1,3,0:T(8,128)} async-done(((f32[32,6,128,128]{2,1,3,0:T(8,128)}), f32[4,6,128,128]{2,1,3,0:T(8,128)}) %reduce-scatter.3.cloned.1.call-update) | async-done | bytes 1572880 | tf_op jit(solution)/shard_map/reduce_scatter | solution.py:139
  358.1 2.0 fusion
  360.1 0.9 all_to_all.68
  361.0 18.2 %all_to_all.77 = bf16[8,64,768]{2,1,0:T(8,128)(2,1)S(1)} all-to-all(bf16[8,64,768]{2,1,0:T(8,128)(2,1)S(1)} %all_to_all.68), channel_id=1, replica_groups=mesh['cfg'=2,'blk'=8,'uly'=8] {'uly'}, dimensions={0} | all-to-all | bytes 1572864 | tf_op jit(solution)/shard_map/all_to_all | solution.py:143
  379.2 0.9 copy.36
  (24 shorter events, 0.3 us)
Async XLA Ops:
  6.5 27.1 %copy-start = (s32[32,96]{1,0:T(8,128)S(1)}, s32[32,96]{1,0:T(8,128)}, u32[]{:S(2)}) copy-start(s32[32,96]{1,0:T(8,128)} %param.11) | copy-start | bytes 36868
  6.5 20.3 %copy-start.5 = (bf16[64,6144]{1,0:T(8,128)(2,1)S(1)}, bf16[64,6144]{1,0:T(8,128)(2,1)}, u32[]{:S(2)}) copy-start(bf16[64,6144]{1,0:T(8,128)(2,1)} %param.7) | copy-start | bytes 2359300
  6.5 61.7 %all-gather.2.cloned.1.call-start = ((), (), s32[]{:S(2)}) async-start(), calls=%async_computation.6 | async-start | bytes 7077888 | tf_op jit(solution)/shard_map/all_gather | solution.py:123
  26.8 7.4 %copy-start.6 = (bf16[64,6144]{1,0:T(8,128)(2,1)S(1)}, bf16[64,6144]{1,0:T(8,128)(2,1)}, u32[]{:S(2)}) copy-start(bf16[64,6144]{1,0:T(8,128)(2,1)} %param.8) | copy-start | bytes 2359300
  27.8 16.1 %all-to-all-start.1 = ((bf16[64,8,768]{2,0,1:T(8,128)(2,1)}), bf16[64,8,768]{2,0,1:T(8,128)(2,1)S(1)}, u32[]{:S(2)}, u32[]{:S(2)}) async-start(bf16[64,8,768]{2,0,1:T(8,128)(2,1)} %bitcast.26), calls=%async_computation.1 | async-start | bytes 1572864 | tf_op jit(solution)/shard_map/all_to_all | solution.py:124
  43.8 16.8 %all-to-all-start.2 = ((bf16[64,8,768]{2,0,1:T(8,128)(2,1)}), bf16[64,8,768]{2,0,1:T(8,128)(2,1)}, u32[]{:S(2)}, u32[]{:S(2)}) async-start(bf16[64,8,768]{2,0,1:T(8,128)(2,1)} %bitcast.25), calls=%async_computation.2 | async-start | bytes 1572864 | tf_op jit(solution)/shard_map/all_to_all | solution.py:125
  49.8 183.3 %all-reduce.2.cloned.1.call-start = ((), (), s32[]{:S(2)}) async-start(), calls=%async_computation.7 | async-start | bytes 262144 | tf_op jit(solution)/shard_map/pmax | solution.py:135
  68.3 1.7 copy-start.3
  161.6 2.7 copy-start.2
  164.3 100.8 %reduce-scatter.5.cloned.1.call-start = ((), (), s32[]{:S(2)}) async-start(), calls=%async_computation.9 | async-start | bytes 147456 | tf_op jit(solution)/shard_map/reduce_scatter | solution.py:140
  234.2 0.7 copy-start.4
  234.8 123.3 %reduce-scatter.3.cloned.1.call-start = ((), (), s32[]{:S(2)}) async-start(), calls=%async_computation.8 | async-start | bytes 18874368 | tf_op jit(solution)/shard_map/reduce_scatter | solution.py:139
  358.1 22.0 %copy-start.1 = (s32[32,96]{1,0:T(8,128)S(1)}, s32[32,96]{1,0:T(8,128)}, u32[]{:S(2)}) copy-start(s32[32,96]{1,0:T(8,128)} %param.11) | copy-start | bytes 36868
Sparse Core Ops, SparseCore 0:
  26.9 41.2 all-gather.1
  164.4 68.6 all-reduce.1
  235.6 29.4 reduce-scatter.4
  267.4 90.6 reduce-scatter.2

commit v2 on v1

v2 whole, which is shorter than its diff:
```python
import functools

import jax
import jax.numpy as jnp
from jax import lax
from jax.experimental import pallas as pl
from jax.experimental.pallas import tpu as pltpu
from jax.sharding import PartitionSpec as P

DH = 128
TILE = 128
HEADS = 6
WIDTH = HEADS * DH
ROWS = 144
PIECE = WIDTH + 16
GROUP = 4
PER = 4
LOW = -1e30
LOG2 = 1.4426950408889634 * DH ** (-0.5)
MESH = pl.DeviceIdType.MESH


def split_low(x):
    high = x.astype(jnp.bfloat16).astype(jnp.float32)
    return jnp.concatenate([high, x - high], axis=0).astype(jnp.bfloat16)


def attend_kernel(order_ref, count_ref, q_ref, k_ref, v_ref, o_ref, vt, acc, top):
    step = pl.program_id(0)
    tiles = vt.shape[0]

    @pl.when(step == 0)
    def _():
        def turn(t, carry):
            rows = pl.ds(pl.multiple_of(t * TILE, TILE), TILE)
            for h in range(HEADS):
                vt[t, h * ROWS : h * ROWS + DH, :] = v_ref[rows, h * DH : (h + 1) * DH].T
                vt[t, h * ROWS + DH : (h + 1) * ROWS, :] = jnp.ones((ROWS - DH, TILE), jnp.bfloat16)
            return carry

        lax.fori_loop(0, tiles, turn, 0)
        top[...] = jnp.full_like(top, LOW)

    def one(sub, carry):
        tile = step * PER + sub
        q_rows = pl.ds(pl.multiple_of(sub * TILE, TILE), TILE)
        count = count_ref[tile]

        def scores(h, picked):
            cols = slice(h * DH, (h + 1) * DH)
            ks = [k_ref[pl.ds(pl.multiple_of(t * TILE, TILE), TILE), cols] for t in picked]
            return lax.dot_general(
                jnp.concatenate(ks, axis=0),
                q_ref[q_rows, cols],
                (((1,), (1,)), ((), ())),
                preferred_element_type=jnp.float32,
            )

        def weigh(h, picked, s, first):
            new = jnp.max(s, axis=0, keepdims=True)
            if not first:
                old = top[h : h + 1, :]
                new = jnp.maximum(old, new)
                scale = jnp.exp2((old - new) * LOG2)
            top[h : h + 1, :] = new
            p = jnp.exp2((s - new) * LOG2).astype(jnp.bfloat16)
            vs = jnp.concatenate([vt[t, h * ROWS : (h + 1) * ROWS, :] for t in picked], axis=1)
            got = jnp.dot(vs, p, preferred_element_type=jnp.float32)
            acc[h] = got if first else acc[h] * scale + got

        def visit(picked, first):
            all_scores = [scores(h, picked) for h in range(HEADS)]
            for h in range(HEADS):
                weigh(h, picked, all_scores[h], first)

        def none():
            acc[...] = jnp.zeros_like(acc)

        def lead_visit(n):
            visit([order_ref[tile, a] for a in range(n)], True)

        lead = jnp.where(count == 0, 0, lax.rem(count + GROUP - 1, GROUP) + 1)
        lax.switch(lead, [none] + [functools.partial(lead_visit, n) for n in range(1, GROUP + 1)])

        def more(j, inner):
            visit([order_ref[tile, lead + GROUP * j + a] for a in range(GROUP)], False)
            return inner

        lax.fori_loop(0, (count - lead) // GROUP, more, 0)

        totals = [acc[h, DH : DH + 1, :] for h in range(HEADS)]
        for h in range(HEADS):
            safe = jnp.where(totals[h] > 0, totals[h], 1.0)
            o_ref[sub, h * DH : (h + 1) * DH, :] = (acc[h, :DH, :] * (1.0 / safe)).astype(jnp.bfloat16)
        total = jnp.concatenate(totals + [jnp.zeros((8 - HEADS, TILE), jnp.float32)], axis=0)
        found = total > 0
        lse = jnp.where(found, top[...] * LOG2 + jnp.log2(jnp.where(found, total, 1.0)), LOW)
        o_ref[sub, WIDTH:PIECE, :] = split_low(lse)
        return carry

    lax.fori_loop(0, PER, one, 0)


def attend(order, counts, queries, keys, values):
    steps = queries.shape[0] // TILE
    tiles = keys.shape[0] // TILE
    whole = pl.BlockSpec(keys.shape, lambda i, *_: (0, 0))
    return pl.pallas_call(
        attend_kernel,
        out_shape=jax.ShapeDtypeStruct((steps, PIECE, TILE), jnp.bfloat16),
        grid_spec=pltpu.PrefetchScalarGridSpec(
            num_scalar_prefetch=2,
            grid=(steps // PER,),
            in_specs=[pl.BlockSpec((TILE * PER, WIDTH), lambda i, *_: (i, 0)), whole, whole],
            out_specs=pl.BlockSpec((PER, PIECE, TILE), lambda i, *_: (i, 0, 0)),
            scratch_shapes=[
                pltpu.VMEM((tiles, HEADS * ROWS, TILE), jnp.bfloat16),
                pltpu.VMEM((HEADS, ROWS, TILE), jnp.float32),
                pltpu.VMEM((8, TILE), jnp.float32),
            ],
        ),
        compiler_params=pltpu.CompilerParams(vmem_limit_bytes=48 * 1024 * 1024),
        cost_estimate=pl.CostEstimate(flops=6 * 10**9, bytes_accessed=18 * 10**6, transcendentals=12 * 10**6),
    )(order, counts, queries, keys, values)


def merge(pieces):
    logs = []
    for ref, at in pieces:
        both = ref[at, WIDTH:PIECE, :].astype(jnp.float32)
        logs.append(both[:8] + both[8:])
    best = functools.reduce(jnp.maximum, logs)
    weights = [jnp.exp2(log - best) for log in logs]
    total = functools.reduce(jnp.add, weights)
    inverse = 1.0 / total
    shares = [w * inverse for w in weights]
    return shares, best + jnp.log2(total)


def head_sum(pieces, shares, h):
    found = None
    for (ref, at), share in zip(pieces, shares):
        term = ref[at, h * DH : (h + 1) * DH, :].astype(jnp.float32) * share[h : h + 1, :]
        found = term if found is None else found + term
    return found


def join_kernel(
    zs, part_ref, out_ref, own, sib, far, near, send_far, send_near, done,
    own_sem, sib_send, sib_recv, far_send, far_recv, near_send, near_recv, out_send, out_recv, out_local,
):
    blk = lax.axis_index("blk")
    uly = lax.axis_index("uly")
    z, core = blk // 2, blk % 2
    ring = [lax.rem(z + d, zs) for d in (2, 1, zs - 1, 0)]
    sibling = {"blk": z * 2 + 1 - core}
    ahead = {"blk": ring[1] * 2 + core}
    behind = {"blk": ring[2] * 2 + core}
    ulys = lax.axis_size("uly")
    tiles = own.shape[1]

    barrier = pltpu.get_barrier_semaphore()
    for device in (sibling, ahead, behind):
        pl.semaphore_signal(barrier, inc=1, device_id=device, device_id_type=MESH)
    for d in range(1, ulys):
        pl.semaphore_signal(barrier, inc=1, device_id={"uly": lax.rem(uly + d, ulys)}, device_id_type=MESH)

    def own_copy(slot, t):
        index = (ring[slot] * 2 + core) * tiles + t
        return pltpu.make_async_copy(part_ref.at[index], own.at[slot, t], own_sem.at[slot, t])

    def sib_copy(slot, t):
        index = (ring[slot] * 2 + 1 - core) * tiles + t
        return pltpu.make_async_remote_copy(
            src_ref=part_ref.at[index], dst_ref=sib.at[slot, t],
            send_sem=sib_send.at[slot, t], recv_sem=sib_recv.at[slot, t],
            device_id=sibling, device_id_type=MESH,
        )

    def far_copy(t):
        return pltpu.make_async_remote_copy(
            src_ref=send_far.at[t], dst_ref=far.at[t],
            send_sem=far_send.at[t], recv_sem=far_recv.at[t],
            device_id=ahead if t < 2 else behind, device_id_type=MESH,
        )

    def near_copy(way, t):
        return pltpu.make_async_remote_copy(
            src_ref=send_near.at[way, t], dst_ref=near.at[way, t],
            send_sem=near_send.at[way, t], recv_sem=near_recv.at[way, t],
            device_id=ahead if way == 0 else behind, device_id_type=MESH,
        )

    order = (
        [(0, 0), (0, 2), (0, 1), (0, 3), (1, 2), (2, 0), (1, 3), (2, 1), (1, 0), (2, 2), (1, 1), (2, 3)]
        + [(3, 0), (3, 2), (3, 1), (3, 3)]
    )
    for slot, t in order:
        own_copy(slot, t).start()
    pl.semaphore_wait(barrier, 3 + ulys - 1)
    for slot, t in order:
        sib_copy(slot, t).start()

    def ready(slot, t):
        own_copy(slot, t).wait()
        sib_copy(slot, t).wait_recv()
        return [(own.at[slot], t), (sib.at[slot], t)]

    def store(pieces, dst):
        shares, log = merge(pieces)
        for h in range(HEADS):
            dst[h * DH : (h + 1) * DH, :] = head_sum(pieces, shares, h).astype(jnp.bfloat16)
        dst[WIDTH:PIECE, :] = split_low(log)

    for t in (0, 2, 1, 3):
        store(ready(0, t), send_far.at[t])
        far_copy(t).start()
    for way, t in ((0, 2), (1, 0), (0, 3), (1, 1)):
        store(ready(way + 1, t), send_near.at[way, t])
        near_copy(way, t).start()
    for way, t in ((0, 0), (1, 2), (0, 1), (1, 3)):
        pieces = ready(way + 1, t)
        far_copy(t).wait_recv()
        store(pieces + [(far, t)], send_near.at[way, t])
        near_copy(way, t).start()

    half = out_ref.shape[0]

    def out_copy(u):
        return pltpu.make_async_remote_copy(
            src_ref=done.at[u], dst_ref=out_ref.at[:, pl.ds(pl.multiple_of(uly * WIDTH, WIDTH), WIDTH)],
            send_sem=out_send.at[u], recv_sem=out_recv.at[uly],
            device_id={"uly": u}, device_id_type=MESH,
        )

    def out_keep(u):
        return pltpu.make_async_copy(
            done.at[u], out_ref.at[:, pl.ds(pl.multiple_of(uly * WIDTH, WIDTH), WIDTH)], out_local
        )

    for t in (0, 2, 1, 3):
        pieces = ready(3, t)
        near_copy(0, t).wait_recv()
        near_copy(1, t).wait_recv()
        pieces = pieces + [(near.at[0], t), (near.at[1], t)]
        shares, log = merge(pieces)
        for h in range(HEADS):
            flat = head_sum(pieces, shares, h).astype(jnp.bfloat16).T
            for j in range(2):
                done[2 * t + j, :, h * DH : (h + 1) * DH] = flat[j * half : (j + 1) * half]
        for j in range(2):
            u = 2 * t + j

            @pl.when(uly != u)
            def _():
                out_copy(u).start()

            @pl.when(uly == u)
            def _():
                out_keep(u).start()

    out_keep(0).wait()
    for u in range(ulys):

        @pl.when(uly != u)
        def _():
            pltpu.make_async_remote_copy(
                src_ref=done.at[u], dst_ref=out_ref.at[:, u * WIDTH : (u + 1) * WIDTH],
                send_sem=out_send.at[u], recv_sem=out_recv.at[u],
                device_id={"uly": u}, device_id_type=MESH,
            ).wait()

    for slot, t in order:
        sib_copy(slot, t).wait_send()
    for t in range(tiles):
        far_copy(t).wait_send()
        near_copy(0, t).wait_send()
        near_copy(1, t).wait_send()


def join(part, rows, zs, ulys):
    tiles = part.shape[0] // (2 * zs)
    piece = (PIECE, TILE)
    dma = pltpu.SemaphoreType.DMA
    return pl.pallas_call(
        functools.partial(join_kernel, zs),
        out_shape=jax.ShapeDtypeStruct((rows, ulys * WIDTH), jnp.bfloat16),
        in_specs=[pl.BlockSpec(memory_space=pl.ANY)],
        out_specs=pl.BlockSpec(memory_space=pl.ANY),
        scratch_shapes=[
            pltpu.VMEM((4, tiles) + piece, jnp.bfloat16),
            pltpu.VMEM((4, tiles) + piece, jnp.bfloat16),
            pltpu.VMEM((tiles,) + piece, jnp.bfloat16),
            pltpu.VMEM((2, tiles) + piece, jnp.bfloat16),
            pltpu.VMEM((tiles,) + piece, jnp.bfloat16),
            pltpu.VMEM((2, tiles) + piece, jnp.bfloat16),
            pltpu.VMEM((ulys, rows, WIDTH), jnp.bfloat16),
            dma((4, tiles)), dma((4, tiles)), dma((4, tiles)),
            dma((tiles,)), dma((tiles,)),
            dma((2, tiles)), dma((2, tiles)),
            dma((ulys,)), dma((ulys,)), dma,
        ],
        compiler_params=pltpu.CompilerParams(
            collective_id=1, has_side_effects=True, vmem_limit_bytes=48 * 1024 * 1024
        ),
        cost_estimate=pl.CostEstimate(flops=2 * 10**7, bytes_accessed=10**7, transcendentals=10**5),
    )(part)


def kept_tiles(keep_flags, ctx_tiles, span_tiles, blk, cycle):
    ctx = lax.dynamic_slice_in_dim(keep_flags, blk * ctx_tiles, ctx_tiles, 1)
    span = lax.dynamic_slice_in_dim(keep_flags, cycle * ctx_tiles + blk * span_tiles, span_tiles, 1)
    mine = (jnp.concatenate([ctx, span], axis=1) > 0).astype(jnp.int32)
    n = mine.shape[1]
    place = jnp.cumsum(mine, axis=1) - 1
    slot = jnp.arange(n, dtype=jnp.int32)
    hit = (place[:, :, None] == slot[None, None, :]) & (mine[:, :, None] > 0)
    order = jnp.sum(jnp.where(hit, slot[None, :, None], 0), axis=1)
    return order, jnp.sum(mine, axis=1)


def shards(new_queries, new_keys, new_values, context_keys, context_values, keep_flags):
    span_queries = lax.all_to_all(new_queries, "uly", split_axis=1, concat_axis=0, tiled=True)
    queries = lax.all_gather(span_queries, "blk", axis=0, tiled=True)
    span_keys = lax.all_to_all(new_keys, "uly", split_axis=1, concat_axis=0, tiled=True)
    span_values = lax.all_to_all(new_values, "uly", split_axis=1, concat_axis=0, tiled=True)
    keys = jnp.concatenate([context_keys, span_keys], axis=0)
    values = jnp.concatenate([context_values, span_values], axis=0)
    cycle = lax.axis_size("blk")
    blk = lax.axis_index("blk")
    order, counts = kept_tiles(
        keep_flags, context_keys.shape[0] // TILE, span_keys.shape[0] // TILE, blk, cycle
    )
    part = attend(order, counts, queries, keys, values)
    return join(part, new_queries.shape[0], cycle // 2, lax.axis_size("uly"))


def solution(mesh):
    in_specs = (
        P(("cfg", "blk", "uly"), None),
        P(("cfg", "blk", "uly"), None),
        P(("cfg", "blk", "uly"), None),
        P(("cfg", "blk"), "uly"),
        P(("cfg", "blk"), "uly"),
        P(),
    )
    out_specs = P(("cfg", "blk", "uly"), None)
    return jax.shard_map(shards, mesh=mesh, in_specs=in_specs, out_specs=out_specs, check_vma=False)
```

time: 390 us -> 157 us (0.40)
  waiting for transfers between devices: 186 us -> 21.9 us
  other arithmetic: 23.7 us -> 5.35 us
  blocking collectives: 37.2 us -> 19 us
  local copies, waits for them, and re-layouts: 22.9 us -> 6.1 us
  Pallas kernels: 91.7 us -> 78.6 us
    reduce_scatter x2 -> x0, waiting for transfers between devices: 107 us -> none  [the longest x1 92.1 us: shards(): weighted = lax.psum_scatter(scaled, 'blk', scatter_dimension=0, tiled=True)]
    pmax x1 -> x0, waiting for transfers between devices: 57.2 us -> none  [shards(): best = lax.pmax(lse, 'blk')]
    all_to_all x1 -> x0, blocking collectives: 18.2 us -> none  [shards(): lax.all_to_all(attended, 'uly', split_axis=0, concat_axis=1, tiled=True)]
    mul x1 -> x0, other arithmetic: 15.3 us -> none  [shards(): part.reshape(steps, HEADS, DH, TILE).astype(jnp.float32)]
    pallas_call x1 -> x2, Pallas kernels: 91.7 us -> 78.6 us  [the longest x1 46.2 us: join(): pl.pallas_call(functools.partial(join_kernel, zs), out_shape=jax.ShapeDty...]
    convert_element_type x1 -> x0, local copies, waits for them, and re-layouts: 11.6 us -> none  [shards(): part.reshape(steps, HEADS, DH, TILE).astype(jnp.float32)]
  transfers between devices with their start and end apart: 6 -> 3, of which waited for: 6 -> 3; matrix products, arithmetic and copies ran while one was open for 9% -> 5% of each run, Pallas kernels for 0% -> 0%
where the time goes in v2:
time: 157 us; the launch traced here: 156 us
  Pallas kernels  78.6 us (50%)
  waiting for transfers between devices  21.9 us (14%)
  blocking collectives  19 us (12%)
  between operations  13.4 us (9%)
  starting transfers between devices  11.9 us (8%)
  local copies, waits for them, and re-layouts  6.1 us (4%)
  other arithmetic  5.35 us (3%)
    pallas_call x1, Pallas kernels, join(): pl.pallas_call(functools.partial(join_kernel, zs), out_shape=jax.ShapeDty...  46.2 us
    pallas_call x1, Pallas kernels, attend(): pl.pallas_call(attend_kernel, out_shape=jax.ShapeDtypeStruct((steps, PIEC...  32.4 us
    all_to_all x1, blocking collectives, shards(): lax.all_to_all(new_queries, 'uly', split_axis=1, concat_axis=0, tiled=True)  19 us
    all_to_all x1, waiting for transfers between devices, shards(): lax.all_to_all(new_values, 'uly', split_axis=1, concat_axis=0, tiled=True)  8.92 us
    all_to_all x1, waiting for transfers between devices, shards(): lax.all_to_all(new_keys, 'uly', split_axis=1, concat_axis=0, tiled=True)  8.63 us
    all_to_all x1, starting transfers between devices, shards(): lax.all_to_all(new_keys, 'uly', split_axis=1, concat_axis=0, tiled=True)  6.01 us
    all_to_all x1, starting transfers between devices, shards(): lax.all_to_all(new_values, 'uly', split_axis=1, concat_axis=0, tiled=True)  5.88 us
    all_gather x1, waiting for transfers between devices, shards(): queries = lax.all_gather(span_queries, 'blk', axis=0, tiled=True)  4.35 us
  transfers between devices with their start and end apart: 3, of which 3 were waited for; matrix products, arithmetic and copies ran while one was open for 5% of the time, Pallas kernels for 0%

profile of v2, /device:TPU:24, one launch (start us, length us, event | category | flops | bytes accessed | tf_op | source)
XLA Modules:
  0.0 156.3 jit_solution(6186270644893869373)
XLA Ops:
  6.5 0.0 copy-start
  6.5 0.0 copy-start.2
  6.5 0.0 all-gather.2.cloned.1.call-start
  6.5 1.3 copy.24
  7.8 19.0 %all_to_all.57 = bf16[64,8,768]{2,0,1:T(8,128)(2,1)} all-to-all(bf16[64,8,768]{2,0,1:T(8,128)(2,1)S(1)} %bitcast.23), channel_id=1, replica_groups=mesh['cfg'=2,'blk'=8,'uly'=8] {'uly'}, dimensions={1} | all-to-all | bytes 1572864 | tf_op jit(solution)/shard_map/all_to_all | solution.py:323
  26.8 0.0 copy-start.3
  26.8 0.0 all-gather.2.cloned.1.call-update
  26.8 0.0 copy-done.2
  26.8 0.9 copy.22
  27.8 5.9 %all-to-all-start.2 = ((bf16[64,8,768]{2,0,1:T(8,128)(2,1)}), bf16[64,8,768]{2,0,1:T(8,128)(2,1)S(1)}, u32[]{:S(2)}, u32[]{:S(2)}) async-start(bf16[64,8,768]{2,0,1:T(8,128)(2,1)} %bitcast.18), calls=%async_computation.2 | async-start | bytes 1572864 | tf_op jit(solution)/shard_map/all_to_all | solution.py:326
  33.6 0.0 copy-done.3
  33.6 0.9 copy.23
  34.6 0.0 copy-done
  34.6 0.1 constant_dynamic-slice_fusion
  34.7 0.1 constant_dynamic-slice_fusion.1
  34.7 0.2 fusion.2
  34.9 8.9 %all-to-all-done.2 = bf16[64,8,768]{2,0,1:T(8,128)(2,1)S(1)} async-done(((bf16[64,8,768]{2,0,1:T(8,128)(2,1)}), bf16[64,8,768]{2,0,1:T(8,128)(2,1)S(1)}, u32[]{:S(2)}, u32[]{:S(2)}) %all-to-all-start.2) | async-done | bytes 786464 | tf_op jit(solution)/shard_map/all_to_all | solution.py:326
  43.8 6.0 %all-to-all-start.1 = ((bf16[64,8,768]{2,0,1:T(8,128)(2,1)}), bf16[64,8,768]{2,0,1:T(8,128)(2,1)}, u32[]{:S(2)}, u32[]{:S(2)}) async-start(bf16[64,8,768]{2,0,1:T(8,128)(2,1)} %bitcast.19), calls=%async_computation.1 | async-start | bytes 1572864 | tf_op jit(solution)/shard_map/all_to_all | solution.py:325
  49.9 0.2 reduce_window_sum.11
  50.0 0.1 copy.11
  50.1 0.1 copy.10
  50.3 0.1 copy.15.order_ref
  50.3 1.7 %pad_maximum_fusion.1.v_ref = bf16[1536,768]{1,0:T(8,128)(2,1)S(1)} fusion(bf16[512,768]{1,0:T(8,128)(2,1)S(1)} %bitcast.21, bf16[1024,768]{1,0:T(8,128)(2,1)} %param.10), kind=kLoop, calls=%fused_computation.1 | loop fusion | flops 4718592 | bytes 4718592 | tf_op jit(solution)/shard_map/concatenate | solution.py:328
  52.0 8.6 %all-to-all-done.1 = bf16[64,8,768]{2,0,1:T(8,128)(2,1)} async-done(((bf16[64,8,768]{2,0,1:T(8,128)(2,1)}), bf16[64,8,768]{2,0,1:T(8,128)(2,1)}, u32[]{:S(2)}, u32[]{:S(2)}) %all-to-all-start.1) | async-done | bytes 786464 | tf_op jit(solution)/shard_map/all_to_all | solution.py:325
  60.6 3.3 %pad_maximum_fusion.k_ref = bf16[1536,768]{1,0:T(8,128)(2,1)} fusion(bf16[512,768]{1,0:T(8,128)(2,1)} %bitcast.3, bf16[1024,768]{1,0:T(8,128)(2,1)} %param.9), kind=kLoop, calls=%fused_computation | loop fusion | flops 4718592 | bytes 4718592 | tf_op jit(solution)/shard_map/concatenate | solution.py:327
  63.9 4.3 %all-gather.2.cloned.1.call-done.q_ref = bf16[4096,768]{1,0:T(8,128)(2,1)} async-done(((bf16[512,768]{1,0:T(8,128)(2,1)}), bf16[4096,768]{1,0:T(8,128)(2,1)}) %all-gather.2.cloned.1.call-update) | async-done | bytes 6291472 | tf_op jit(solution)/shard_map/all_gather | solution.py:324
  68.3 0.0 copy-start.1
  68.3 1.7 %copy-done.1 = bf16[1536,768]{1,0:T(8,128)(2,1)S(1)} copy-done((bf16[1536,768]{1,0:T(8,128)(2,1)S(1)}, bf16[1536,768]{1,0:T(8,128)(2,1)}, u32[]{:S(2)}) %copy-start.1) | copy-done | bytes 2359320
  69.9 32.4 %shard_map.64.part_ref = bf16[32,784,128]{2,1,0:T(8,128)(2,1)} custom-call(s32[32,12]{1,0:T(8,128)S(1)} %copy.15.order_ref, s32[32]{0:T(128)S(1)} %get-tuple-element.5.count_ref, bf16[4096,768]{1,0:T(8,128)(2,1)} %all-gather.2.cloned.1.call-done.q_ref, bf16[1536,768]{1,0:T(8,128)(2,1)S(1)} %copy-done.1, bf16[1536,768]{1,0:T(8,128)(2,1)S(1)} %pad_maximum_fusion.1.v_ref), custom_call_target="tpu_custom_call" | custom-call | flops 6000000000 | bytes 18000000 | tf_op jit(solution)/shard_map/pallas_call | solution.py:108
  102.3 46.2 %shard_map.65 = bf16[64,6144]{1,0:T(8,128)(2,1)S(1)} custom-call(bf16[32,784,128]{2,1,0:T(8,128)(2,1)} %shard_map.64.part_ref), custom_call_target="tpu_custom_call" | custom-call | flops 20000000 | bytes 10000000 | tf_op jit(solution)/shard_map/pallas_call | solution.py:285
  148.6 0.9 copy.26
  (3 shorter events, 0.0 us)
Async XLA Ops:
  6.5 28.1 %copy-start = (s32[32,96]{1,0:T(8,128)S(1)}, s32[32,96]{1,0:T(8,128)}, u32[]{:S(2)}) copy-start(s32[32,96]{1,0:T(8,128)} %param.11) | copy-start | bytes 36868
  6.5 20.3 %copy-start.2 = (bf16[64,6144]{1,0:T(8,128)(2,1)S(1)}, bf16[64,6144]{1,0:T(8,128)(2,1)}, u32[]{:S(2)}) copy-start(bf16[64,6144]{1,0:T(8,128)(2,1)} %param.8) | copy-start | bytes 2359300
  6.5 61.7 %all-gather.2.cloned.1.call-start = ((), (), s32[]{:S(2)}) async-start(), calls=%async_computation.3 | async-start | bytes 7077888 | tf_op jit(solution)/shard_map/all_gather | solution.py:324
  26.8 6.9 %copy-start.3 = (bf16[64,6144]{1,0:T(8,128)(2,1)S(1)}, bf16[64,6144]{1,0:T(8,128)(2,1)}, u32[]{:S(2)}) copy-start(bf16[64,6144]{1,0:T(8,128)(2,1)} %param.7) | copy-start | bytes 2359300
  27.8 16.1 %all-to-all-start.2 = ((bf16[64,8,768]{2,0,1:T(8,128)(2,1)}), bf16[64,8,768]{2,0,1:T(8,128)(2,1)S(1)}, u32[]{:S(2)}, u32[]{:S(2)}) async-start(bf16[64,8,768]{2,0,1:T(8,128)(2,1)} %bitcast.18), calls=%async_computation.2 | async-start | bytes 1572864 | tf_op jit(solution)/shard_map/all_to_all | solution.py:326
  43.8 16.8 %all-to-all-start.1 = ((bf16[64,8,768]{2,0,1:T(8,128)(2,1)}), bf16[64,8,768]{2,0,1:T(8,128)(2,1)}, u32[]{:S(2)}, u32[]{:S(2)}) async-start(bf16[64,8,768]{2,0,1:T(8,128)(2,1)} %bitcast.19), calls=%async_computation.1 | async-start | bytes 1572864 | tf_op jit(solution)/shard_map/all_to_all | solution.py:325
  68.3 1.7 %copy-start.1 = (bf16[1536,768]{1,0:T(8,128)(2,1)S(1)}, bf16[1536,768]{1,0:T(8,128)(2,1)}, u32[]{:S(2)}) copy-start(bf16[1536,768]{1,0:T(8,128)(2,1)} %pad_maximum_fusion.k_ref) | copy-start | bytes 7077892
Sparse Core Ops, SparseCore 0:
  26.9 41.2 all-gather.1

commit v3 on v2

--- a/solution.py
+++ b/solution.py
@@ -25,12 +25,30 @@
     return jnp.concatenate([high, x - high], axis=0).astype(jnp.bfloat16)
 
 
-def attend_kernel(order_ref, count_ref, q_ref, k_ref, v_ref, o_ref, vt, acc, top):
+def attend_kernel(
+    blk_ref, flags_ref, q_ref, ck_ref, sk_ref, cv_ref, sv_ref, o_ref, k_ref, v_ref, vt, acc, top, order_ref, sems
+):
     step = pl.program_id(0)
     tiles = vt.shape[0]
+    ctx_rows = ck_ref.shape[0]
+    ctx_tiles = ctx_rows // TILE
+    span_tiles = tiles - ctx_tiles
+    blk = blk_ref[0]
+    first_span = flags_ref.shape[1] - flags_ref.shape[0]
 
     @pl.when(step == 0)
     def _():
+        copies = [
+            pltpu.make_async_copy(cv_ref, v_ref.at[:ctx_rows], sems.at[0]),
+            pltpu.make_async_copy(sv_ref, v_ref.at[ctx_rows:], sems.at[1]),
+            pltpu.make_async_copy(ck_ref, k_ref.at[:ctx_rows], sems.at[2]),
+            pltpu.make_async_copy(sk_ref, k_ref.at[ctx_rows:], sems.at[3]),
+        ]
+        for copy in copies:
+            copy.start()
+        copies[0].wait()
+        copies[1].wait()
+
         def turn(t, carry):
             rows = pl.ds(pl.multiple_of(t * TILE, TILE), TILE)
             for h in range(HEADS):
@@ -40,11 +58,17 @@
 
         lax.fori_loop(0, tiles, turn, 0)
         top[...] = jnp.full_like(top, LOW)
+        copies[2].wait()
+        copies[3].wait()
 
     def one(sub, carry):
         tile = step * PER + sub
         q_rows = pl.ds(pl.multiple_of(sub * TILE, TILE), TILE)
-        count = count_ref[tile]
+        count = jnp.int32(0)
+        for t in range(tiles):
+            column = blk * ctx_tiles + t if t < ctx_tiles else first_span + blk * span_tiles + t - ctx_tiles
+            order_ref[count] = t
+            count = count + jnp.where(flags_ref[tile, column] > 0, 1, 0)
 
         def scores(h, picked):
             cols = slice(h * DH, (h + 1) * DH)
@@ -77,13 +101,13 @@
             acc[...] = jnp.zeros_like(acc)
 
         def lead_visit(n):
-            visit([order_ref[tile, a] for a in range(n)], True)
+            visit([order_ref[a] for a in range(n)], True)
 
         lead = jnp.where(count == 0, 0, lax.rem(count + GROUP - 1, GROUP) + 1)
         lax.switch(lead, [none] + [functools.partial(lead_visit, n) for n in range(1, GROUP + 1)])
 
         def more(j, inner):
-            visit([order_ref[tile, lead + GROUP * j + a] for a in range(GROUP)], False)
+            visit([order_ref[lead + GROUP * j + a] for a in range(GROUP)], False)
             return inner
 
         lax.fori_loop(0, (count - lead) // GROUP, more, 0)
@@ -101,27 +125,184 @@
     lax.fori_loop(0, PER, one, 0)
 
 
-def attend(order, counts, queries, keys, values):
+def attend(blk, flags, queries, context_keys, span_keys, context_values, span_values):
     steps = queries.shape[0] // TILE
-    tiles = keys.shape[0] // TILE
-    whole = pl.BlockSpec(keys.shape, lambda i, *_: (0, 0))
+    rows = context_keys.shape[0] + span_keys.shape[0]
+    tiles = rows // TILE
+    anywhere = pl.BlockSpec(memory_space=pl.ANY)
     return pl.pallas_call(
         attend_kernel,
         out_shape=jax.ShapeDtypeStruct((steps, PIECE, TILE), jnp.bfloat16),
         grid_spec=pltpu.PrefetchScalarGridSpec(
             num_scalar_prefetch=2,
             grid=(steps // PER,),
-            in_specs=[pl.BlockSpec((TILE * PER, WIDTH), lambda i, *_: (i, 0)), whole, whole],
+            in_specs=[pl.BlockSpec((TILE * PER, WIDTH), lambda i, *_: (i, 0))] + [anywhere] * 4,
             out_specs=pl.BlockSpec((PER, PIECE, TILE), lambda i, *_: (i, 0, 0)),
             scratch_shapes=[
+                pltpu.VMEM((rows, WIDTH), jnp.bfloat16),
+                pltpu.VMEM((rows, WIDTH), jnp.bfloat16),
                 pltpu.VMEM((tiles, HEADS * ROWS, TILE), jnp.bfloat16),
                 pltpu.VMEM((HEADS, ROWS, TILE), jnp.float32),
                 pltpu.VMEM((8, TILE), jnp.float32),
+                pltpu.SMEM((tiles,), jnp.int32),
+                pltpu.SemaphoreType.DMA((4,)),
             ],
         ),
         compiler_params=pltpu.CompilerParams(vmem_limit_bytes=48 * 1024 * 1024),
         cost_estimate=pl.CostEstimate(flops=6 * 10**9, bytes_accessed=18 * 10**6, transcendentals=12 * 10**6),
-    )(order, counts, queries, keys, values)
+    )(blk, flags, queries, context_keys, span_keys, context_values, span_values)
+
+
+def spread_kernel(
+    zs, nq_ref, nk_ref, nv_ref, q_ref, k_ref, v_ref,
+    keep_sem, q_send, q_recv, kv_send, kv_recv, own_send, ring_recv, pass_send, far_recv, sib_send, sib_recv,
+):
+    blk = lax.axis_index("blk")
+    uly = lax.axis_index("uly")
+    ulys = lax.axis_size("uly")
+    z, core = blk // 2, blk % 2
+    sibling = {"blk": z * 2 + 1 - core}
+    ahead = {"blk": lax.rem(z + 1, zs) * 2 + core}
+    behind = {"blk": lax.rem(z + zs - 1, zs) * 2 + core}
+    height = nq_ref.shape[0]
+
+    barrier = pltpu.get_barrier_semaphore()
+    for d in range(1, ulys):
+        pl.semaphore_signal(barrier, inc=1, device_id={"uly": lax.rem(uly + d, ulys)}, device_id_type=MESH)
+    for device in (sibling, ahead, behind):
+        pl.semaphore_signal(barrier, inc=1, device_id=device, device_id_type=MESH)
+
+    def columns(u):
+        return pl.ds(pl.multiple_of(u * WIDTH, WIDTH), WIDTH)
+
+    def span_rows(u):
+        return pl.ds(pl.multiple_of(u * height, height), height)
+
+    def q_rows(chip, side, d):
+        source = lax.rem(uly + ulys - d, ulys)
+        return pl.ds(pl.multiple_of(((chip * 2 + side) * ulys + source) * height, height), height)
+
+    def q_copy(d):
+        target = lax.rem(uly + d, ulys)
+        return pltpu.make_async_remote_copy(
+            src_ref=nq_ref.at[:, columns(target)], dst_ref=q_ref.at[q_rows(z, core, 0), :],
+            send_sem=q_send.at[d], recv_sem=q_recv.at[d], device_id={"uly": target}, device_id_type=MESH,
+        )
+
+    def kv_copy(which, d):
+        target = lax.rem(uly + d, ulys)
+        src, dst = ((nk_ref, k_ref), (nv_ref, v_ref))[which]
+        return pltpu.make_async_remote_copy(
+            src_ref=src.at[:, columns(target)], dst_ref=dst.at[span_rows(uly), :],
+            send_sem=kv_send.at[which, d], recv_sem=kv_recv.at[which, d],
+            device_id={"uly": target}, device_id_type=MESH,
+        )
+
+    def kv_wait(which, d):
+        src, dst = ((nk_ref, k_ref), (nv_ref, v_ref))[which]
+        return pltpu.make_async_remote_copy(
+            src_ref=src.at[:, columns(uly)], dst_ref=dst.at[span_rows(lax.rem(uly + ulys - d, ulys)), :],
+            send_sem=kv_send.at[which, d], recv_sem=kv_recv.at[which, d],
+            device_id={"uly": lax.rem(uly + d, ulys)}, device_id_type=MESH,
+        )
+
+    def move(rows, send, recv, device):
+        return pltpu.make_async_remote_copy(
+            src_ref=q_ref.at[rows, :], dst_ref=q_ref.at[rows, :],
+            send_sem=send, recv_sem=recv, device_id=device, device_id_type=MESH,
+        )
+
+    chips = [z, lax.rem(z + zs - 1, zs), lax.rem(z + 1, zs), lax.rem(z + 2, zs)]
+
+    def to_sibling(slot, d):
+        return move(q_rows(chips[slot], core, d), sib_send.at[slot, d], sib_recv.at[slot, d], sibling)
+
+    def from_sibling(slot, d):
+        return move(q_rows(chips[slot], 1 - core, d), sib_send.at[slot, d], sib_recv.at[slot, d], sibling)
+
+    def to_ring(way, d):
+        return move(q_rows(z, core, d), own_send.at[way, d], ring_recv.at[way, d], (ahead, behind)[way])
+
+    def from_ring(way, d):
+        return move(q_rows(chips[1 + way], core, d), own_send.at[way, d], ring_recv.at[way, d], (ahead, behind)[way])
+
+    def onward(way, d):
+        return move(q_rows(chips[1 + way], core, d), pass_send.at[d], far_recv.at[d], (ahead, behind)[way])
+
+    def from_far(d):
+        return move(q_rows(chips[3], core, d), pass_send.at[d], far_recv.at[d], (ahead, behind)[d % 2])
+
+    keeps = [
+        pltpu.make_async_copy(nq_ref.at[:, columns(uly)], q_ref.at[q_rows(z, core, 0), :], keep_sem.at[0]),
+        pltpu.make_async_copy(nk_ref.at[:, columns(uly)], k_ref.at[span_rows(uly), :], keep_sem.at[1]),
+        pltpu.make_async_copy(nv_ref.at[:, columns(uly)], v_ref.at[span_rows(uly), :], keep_sem.at[2]),
+    ]
+    keeps[0].start()
+    pl.semaphore_wait(barrier, ulys - 1 + 3)
+    for d in range(1, ulys):
+        q_copy(d).start()
+    keeps[1].start()
+    keeps[2].start()
+
+    for d in range(ulys):
+        if d == 0:
+            keeps[0].wait()
+        else:
+            move(q_rows(z, core, d), q_send.at[d], q_recv.at[d], sibling).wait_recv()
+        to_ring(0, d).start()
+        to_ring(1, d).start()
+        to_sibling(0, d).start()
+    for which in range(2):
+        for d in range(1, ulys):
+            kv_copy(which, d).start()
+    for d in range(ulys):
+        for way in range(2):
+            from_ring(way, d).wait_recv()
+            if d % 2 == way:
+                onward(way, d).start()
+            to_sibling(1 + way, d).start()
+    for d in range(ulys):
+        from_far(d).wait_recv()
+        to_sibling(3, d).start()
+
+    for d in range(1, ulys):
+        q_copy(d).wait_send()
+        for which in range(2):
+            kv_copy(which, d).wait_send()
+            kv_wait(which, d).wait_recv()
+    keeps[1].wait()
+    keeps[2].wait()
+    for d in range(ulys):
+        to_ring(0, d).wait_send()
+        to_ring(1, d).wait_send()
+        onward(d % 2, d).wait_send()
+        for slot in range(4):
+            to_sibling(slot, d).wait_send()
+            from_sibling(slot, d).wait_recv()
+
+
+def spread(new_queries, new_keys, new_values, zs, ulys):
+    height = new_queries.shape[0]
+    dma = pltpu.SemaphoreType.DMA
+    anywhere = pl.BlockSpec(memory_space=pl.ANY)
+    span = jax.ShapeDtypeStruct((height * ulys, WIDTH), jnp.bfloat16)
+    return pl.pallas_call(
+        functools.partial(spread_kernel, zs),
+        out_shape=(jax.ShapeDtypeStruct((height * ulys * zs * 2, WIDTH), jnp.bfloat16), span, span),
+        in_specs=[anywhere] * 3,
+        out_specs=(anywhere,) * 3,
+        scratch_shapes=[
+            dma((3,)), dma((ulys,)), dma((ulys,)),
+            dma((2, ulys)), dma((2, ulys)),
+            dma((2, ulys)), dma((2, ulys)),
+            dma((ulys,)), dma((ulys,)),
+            dma((4, ulys)), dma((4, ulys)),
+        ],
+        compiler_params=pltpu.CompilerParams(
+            collective_id=0, has_side_effects=True, vmem_limit_bytes=48 * 1024 * 1024
+        ),
+        cost_estimate=pl.CostEstimate(flops=0, bytes_accessed=2 * 10**7, transcendentals=0),
+    )(new_queries, new_keys, new_values)
 
 
 def merge(pieces):
@@ -307,32 +488,12 @@
     )(part)
 
 
-def kept_tiles(keep_flags, ctx_tiles, span_tiles, blk, cycle):
-    ctx = lax.dynamic_slice_in_dim(keep_flags, blk * ctx_tiles, ctx_tiles, 1)
-    span = lax.dynamic_slice_in_dim(keep_flags, cycle * ctx_tiles + blk * span_tiles, span_tiles, 1)
-    mine = (jnp.concatenate([ctx, span], axis=1) > 0).astype(jnp.int32)
-    n = mine.shape[1]
-    place = jnp.cumsum(mine, axis=1) - 1
-    slot = jnp.arange(n, dtype=jnp.int32)
-    hit = (place[:, :, None] == slot[None, None, :]) & (mine[:, :, None] > 0)
-    order = jnp.sum(jnp.where(hit, slot[None, :, None], 0), axis=1)
-    return order, jnp.sum(mine, axis=1)
-
-
 def shards(new_queries, new_keys, new_values, context_keys, context_values, keep_flags):
-    span_queries = lax.all_to_all(new_queries, "uly", split_axis=1, concat_axis=0, tiled=True)
-    queries = lax.all_gather(span_queries, "blk", axis=0, tiled=True)
-    span_keys = lax.all_to_all(new_keys, "uly", split_axis=1, concat_axis=0, tiled=True)
-    span_values = lax.all_to_all(new_values, "uly", split_axis=1, concat_axis=0, tiled=True)
-    keys = jnp.concatenate([context_keys, span_keys], axis=0)
-    values = jnp.concatenate([context_values, span_values], axis=0)
-    cycle = lax.axis_size("blk")
-    blk = lax.axis_index("blk")
-    order, counts = kept_tiles(
-        keep_flags, context_keys.shape[0] // TILE, span_keys.shape[0] // TILE, blk, cycle
-    )
-    part = attend(order, counts, queries, keys, values)
-    return join(part, new_queries.shape[0], cycle // 2, lax.axis_size("uly"))
+    zs, ulys = lax.axis_size("blk") // 2, lax.axis_size("uly")
+    queries, span_keys, span_values = spread(new_queries, new_keys, new_values, zs, ulys)
+    blk = jnp.reshape(lax.axis_index("blk").astype(jnp.int32), (1,))
+    part = attend(blk, keep_flags, queries, context_keys, span_keys, context_values, span_values)
+    return join(part, new_queries.shape[0], zs, ulys)
 
 
 def solution(mesh):

time: 157 us -> 126 us (0.80)
  Pallas kernels: 78.6 us -> 118 us
  waiting for transfers between devices: 21.9 us -> 0 us
  blocking collectives: 19 us -> 0 us
  between operations: 13.4 us -> 0.04 us
  starting transfers between devices: 11.9 us -> 0 us
  other arithmetic: 5.35 us -> 0 us
  local copies, waits for them, and re-layouts: 6.1 us -> 7.81 us
    pallas_call x0 -> x1, Pallas kernels: none -> 40.5 us  [spread(): pl.pallas_call(functools.partial(spread_kernel, zs), out_shape=(jax.Shape...]
    all_to_all x1 -> x0, blocking collectives: 19 us -> none  [shards(): lax.all_to_all(new_queries, 'uly', split_axis=1, concat_axis=0, tiled=True)]
    all_to_all x2 -> x0, waiting for transfers between devices: 17.5 us -> none  [the longest x1 8.92 us: shards(): lax.all_to_all(new_values, 'uly', split_axis=1, concat_axis=0, tiled=True)]
    all_to_all x2 -> x0, starting transfers between devices: 11.9 us -> none  [the longest x1 6.01 us: shards(): lax.all_to_all(new_keys, 'uly', split_axis=1, concat_axis=0, tiled=True)]
    unnamed x9 -> x13, local copies, waits for them, and re-layouts: 2.56 us -> 7.81 us
    concatenate x2 -> x0, other arithmetic: 4.95 us -> none  [the longest x1 3.29 us: shards(): keys = jnp.concatenate([context_keys, span_keys], axis=0)]
    all_gather x1 -> x0, waiting for transfers between devices: 4.35 us -> none  [shards(): queries = lax.all_gather(span_queries, 'blk', axis=0, tiled=True)]
    all_to_all x3 -> x0, local copies, waits for them, and re-layouts: 3.14 us -> none  [the longest x1 1.26 us: shards(): lax.all_to_all(new_queries, 'uly', split_axis=1, concat_axis=0, tiled=True)]
  transfers between devices with their start and end apart: 3 -> 0, of which waited for: 3 -> 0; matrix products, arithmetic and copies ran while one was open for 5% -> 0% of each run, Pallas kernels for 0% -> 0%
where the time goes in v3:
time: 126 us
  Pallas kernels  118 us (94%)
  local copies, waits for them, and re-layouts  7.81 us (6%)
    pallas_call x1, Pallas kernels, join(): pl.pallas_call(functools.partial(join_kernel, zs), out_shape=jax.ShapeDty...  45.2 us
    pallas_call x1, Pallas kernels, spread(): pl.pallas_call(functools.partial(spread_kernel, zs), out_shape=(jax.Shape...  40.5 us
    pallas_call x1, Pallas kernels, attend(): pl.pallas_call(attend_kernel, out_shape=jax.ShapeDtypeStruct((steps, PIEC...  32.1 us
    unnamed x13, local copies, waits for them, and re-layouts  7.81 us

profile of v3, /device:TPU:24, one launch (start us, length us, event | category | flops | bytes accessed | tf_op | source)
XLA Modules:
  0.0 125.6 jit_solution(13769861896318012921)
XLA Ops:
  0.0 0.0 copy-start
  0.0 1.1 copy-done
  1.1 0.0 copy-start.1
  1.1 1.1 copy-done.1
  2.3 0.0 copy-start.2
  2.3 1.1 copy-done.2
  3.4 40.5 %shard_map.64 = (bf16[4096,768]{1,0:T(8,128)(2,1)}, bf16[512,768]{1,0:T(8,128)(2,1)S(1)}, bf16[512,768]{1,0:T(8,128)(2,1)S(1)}) custom-call(bf16[64,6144]{1,0:T(8,128)(2,1)S(1)} %copy-done, bf16[64,6144]{1,0:T(8,128)(2,1)S(1)} %copy-done.1, bf16[64,6144]{1,0:T(8,128)(2,1)S(1)} %copy-done.2), custom_call_target="tpu_custom_call" | custom-call | bytes 20000000 | tf_op jit(solution)/shard_map/pallas_call | solution.py:289
  43.9 0.0 copy-start.3
  43.9 1.4 %copy-done.3 = bf16[1024,768]{1,0:T(8,128)(2,1)S(1)} copy-done((bf16[1024,768]{1,0:T(8,128)(2,1)S(1)}, bf16[1024,768]{1,0:T(8,128)(2,1)}, u32[]{:S(2)}) %copy-start.3) | copy-done | bytes 1572888
  45.3 0.0 copy-start.4
  45.3 1.4 %copy-done.4 = bf16[1024,768]{1,0:T(8,128)(2,1)S(1)} copy-done((bf16[1024,768]{1,0:T(8,128)(2,1)S(1)}, bf16[1024,768]{1,0:T(8,128)(2,1)}, u32[]{:S(2)}) %copy-start.4) | copy-done | bytes 1572888
  46.7 0.0 copy-start.5
  46.7 0.7 copy-done.5
  47.4 32.1 %shard_map.65.part_ref = bf16[32,784,128]{2,1,0:T(8,128)(2,1)} custom-call(s32[1]{0:T(128)} %bitcast.blk_ref, s32[32,96]{1,0:T(8,128)S(1)} %copy-done.5, bf16[4096,768]{1,0:T(8,128)(2,1)} %get-tuple-element.8.q_ref, bf16[1024,768]{1,0:T(8,128)(2,1)S(1)} %copy-done.3, bf16[512,768]{1,0:T(8,128)(2,1)S(1)} %get-tuple-element.9.sk_ref, ...), custom_call_target="tpu_custom_call" | custom-call | flops 6000000000 | bytes 18000000 | tf_op jit(solution)/shard_map/pallas_call | solution.py:133
  79.5 45.2 %shard_map.66 = bf16[64,6144]{1,0:T(8,128)(2,1)S(1)} custom-call(bf16[32,784,128]{2,1,0:T(8,128)(2,1)} %shard_map.65.part_ref), custom_call_target="tpu_custom_call" | custom-call | flops 20000000 | bytes 10000000 | tf_op jit(solution)/shard_map/pallas_call | solution.py:466
  124.7 0.9 copy.8
Async XLA Ops:
  0.0 1.1 copy-start
  1.1 1.1 copy-start.1
  2.3 1.1 copy-start.2
  43.9 1.4 %copy-start.3 = (bf16[1024,768]{1,0:T(8,128)(2,1)S(1)}, bf16[1024,768]{1,0:T(8,128)(2,1)}, u32[]{:S(2)}) copy-start(bf16[1024,768]{1,0:T(8,128)(2,1)} %ck_ref.1) | copy-start | bytes 4718596
  45.3 1.4 %copy-start.4 = (bf16[1024,768]{1,0:T(8,128)(2,1)S(1)}, bf16[1024,768]{1,0:T(8,128)(2,1)}, u32[]{:S(2)}) copy-start(bf16[1024,768]{1,0:T(8,128)(2,1)} %cv_ref.1) | copy-start | bytes 4718596
  46.7 0.7 copy-start.5

commit v4 on v3

--- a/solution.py
+++ b/solution.py
@@ -15,6 +15,8 @@
 PIECE = WIDTH + 16
 GROUP = 4
 PER = 4
+VMEM_LIMIT = 62 * 1024 * 1024
+DEPTH = 1
 LOW = -1e30
 LOG2 = 1.4426950408889634 * DH ** (-0.5)
 MESH = pl.DeviceIdType.MESH
@@ -148,13 +150,13 @@
                 pltpu.SemaphoreType.DMA((4,)),
             ],
         ),
-        compiler_params=pltpu.CompilerParams(vmem_limit_bytes=48 * 1024 * 1024),
+        compiler_params=pltpu.CompilerParams(vmem_limit_bytes=VMEM_LIMIT),
         cost_estimate=pl.CostEstimate(flops=6 * 10**9, bytes_accessed=18 * 10**6, transcendentals=12 * 10**6),
     )(blk, flags, queries, context_keys, span_keys, context_values, span_values)
 
 
 def spread_kernel(
-    zs, nq_ref, nk_ref, nv_ref, q_ref, k_ref, v_ref,
+    zs, nq_ref, nk_ref, nv_ref, q_ref, k_ref, v_ref, stage,
     keep_sem, q_send, q_recv, kv_send, kv_recv, own_send, ring_recv, pass_send, far_recv, sib_send, sib_recv,
 ):
     blk = lax.axis_index("blk")
@@ -232,23 +234,38 @@
     def from_far(d):
         return move(q_rows(chips[3], core, d), pass_send.at[d], far_recv.at[d], (ahead, behind)[d % 2])
 
+    fetches = [
+        pltpu.make_async_copy(src.at[:, columns(uly)], stage.at[i], keep_sem.at[i])
+        for i, src in enumerate((nq_ref, nk_ref, nv_ref))
+    ]
     keeps = [
-        pltpu.make_async_copy(nq_ref.at[:, columns(uly)], q_ref.at[q_rows(z, core, 0), :], keep_sem.at[0]),
-        pltpu.make_async_copy(nk_ref.at[:, columns(uly)], k_ref.at[span_rows(uly), :], keep_sem.at[1]),
-        pltpu.make_async_copy(nv_ref.at[:, columns(uly)], v_ref.at[span_rows(uly), :], keep_sem.at[2]),
+        pltpu.make_async_copy(stage.at[i], dst, keep_sem.at[i])
+        for i, dst in enumerate(
+            (q_ref.at[q_rows(z, core, 0), :], k_ref.at[span_rows(uly), :], v_ref.at[span_rows(uly), :])
+        )
     ]
-    keeps[0].start()
+    for fetch in fetches:
+        fetch.start()
+    for fetch in fetches:
+        fetch.wait()
     pl.semaphore_wait(barrier, ulys - 1 + 3)
+
+    def own_piece(send, recv, device):
+        return pltpu.make_async_remote_copy(
+            src_ref=stage.at[0], dst_ref=q_ref.at[q_rows(z, core, 0), :],
+            send_sem=send, recv_sem=recv, device_id=device, device_id_type=MESH,
+        )
+
+    own_piece(own_send.at[0, 0], ring_recv.at[0, 0], ahead).start()
+    own_piece(own_send.at[1, 0], ring_recv.at[1, 0], behind).start()
     for d in range(1, ulys):
         q_copy(d).start()
-    keeps[1].start()
-    keeps[2].start()
-
-    for d in range(ulys):
-        if d == 0:
-            keeps[0].wait()
-        else:
-            move(q_rows(z, core, d), q_send.at[d], q_recv.at[d], sibling).wait_recv()
+    own_piece(sib_send.at[0, 0], sib_recv.at[0, 0], sibling).start()
+    for keep in keeps:
+        keep.start()
+
+    for d in range(1, ulys):
+        move(q_rows(z, core, d), q_send.at[d], q_recv.at[d], sibling).wait_recv()
         to_ring(0, d).start()
         to_ring(1, d).start()
         to_sibling(0, d).start()
@@ -270,8 +287,8 @@
         for which in range(2):
             kv_copy(which, d).wait_send()
             kv_wait(which, d).wait_recv()
-    keeps[1].wait()
-    keeps[2].wait()
+    for keep in keeps:
+        keep.wait()
     for d in range(ulys):
         to_ring(0, d).wait_send()
         to_ring(1, d).wait_send()
@@ -289,9 +306,10 @@
     return pl.pallas_call(
         functools.partial(spread_kernel, zs),
         out_shape=(jax.ShapeDtypeStruct((height * ulys * zs * 2, WIDTH), jnp.bfloat16), span, span),
-        in_specs=[anywhere] * 3,
+        in_specs=[pl.BlockSpec(memory_space=pltpu.HBM)] * 3,
         out_specs=(anywhere,) * 3,
         scratch_shapes=[
+            pltpu.VMEM((3, height, WIDTH), jnp.bfloat16),
             dma((3,)), dma((ulys,)), dma((ulys,)),
             dma((2, ulys)), dma((2, ulys)),
             dma((2, ulys)), dma((2, ulys)),
@@ -299,7 +317,7 @@
             dma((4, ulys)), dma((4, ulys)),
         ],
         compiler_params=pltpu.CompilerParams(
-            collective_id=0, has_side_effects=True, vmem_limit_bytes=48 * 1024 * 1024
+            collective_id=0, has_side_effects=True, vmem_limit_bytes=VMEM_LIMIT
         ),
         cost_estimate=pl.CostEstimate(flops=0, bytes_accessed=2 * 10**7, transcendentals=0),
     )(new_queries, new_keys, new_values)
@@ -346,12 +364,15 @@
     for d in range(1, ulys):
         pl.semaphore_signal(barrier, inc=1, device_id={"uly": lax.rem(uly + d, ulys)}, device_id_type=MESH)
 
+    def turned(t):
+        return lax.rem(t + uly, tiles)
+
     def own_copy(slot, t):
-        index = (ring[slot] * 2 + core) * tiles + t
+        index = (ring[slot] * 2 + core) * tiles + turned(t)
         return pltpu.make_async_copy(part_ref.at[index], own.at[slot, t], own_sem.at[slot, t])
 
     def sib_copy(slot, t):
-        index = (ring[slot] * 2 + 1 - core) * tiles + t
+        index = (ring[slot] * 2 + 1 - core) * tiles + turned(t)
         return pltpu.make_async_remote_copy(
             src_ref=part_ref.at[index], dst_ref=sib.at[slot, t],
             send_sem=sib_send.at[slot, t], recv_sem=sib_recv.at[slot, t],
@@ -372,10 +393,9 @@
             device_id=ahead if way == 0 else behind, device_id_type=MESH,
         )
 
-    order = (
-        [(0, 0), (0, 2), (0, 1), (0, 3), (1, 2), (2, 0), (1, 3), (2, 1), (1, 0), (2, 2), (1, 1), (2, 3)]
-        + [(3, 0), (3, 2), (3, 1), (3, 3)]
-    )
+    order = [(0, 0), (0, 2), (0, 1), (0, 3)]
+    order += [(slot, t) for t in (0, 2, 1, 3) for slot in (1, 2)]
+    order += [(3, t) for t in (0, 2, 1, 3)]
     for slot, t in order:
         own_copy(slot, t).start()
     pl.semaphore_wait(barrier, 3 + ulys - 1)
@@ -396,27 +416,31 @@
     for t in (0, 2, 1, 3):
         store(ready(0, t), send_far.at[t])
         far_copy(t).start()
-    for way, t in ((0, 2), (1, 0), (0, 3), (1, 1)):
-        store(ready(way + 1, t), send_near.at[way, t])
-        near_copy(way, t).start()
-    for way, t in ((0, 0), (1, 2), (0, 1), (1, 3)):
-        pieces = ready(way + 1, t)
-        far_copy(t).wait_recv()
-        store(pieces + [(far, t)], send_near.at[way, t])
-        near_copy(way, t).start()
+    for t in (0, 2, 1, 3):
+        passed = t // 2
+        for way in (1 - passed, passed):
+            pieces = ready(way + 1, t)
+            if way == passed:
+                far_copy(t).wait_recv()
+                pieces = pieces + [(far, t)]
+            place = (0, 2, 1, 3).index(t)
+            store(pieces, send_near.at[way, t])
+            if place >= DEPTH:
+                near_copy(way, (0, 2, 1, 3)[place - DEPTH]).wait_send()
+            near_copy(way, t).start()
 
     half = out_ref.shape[0]
 
-    def out_copy(u):
-        return pltpu.make_async_remote_copy(
-            src_ref=done.at[u], dst_ref=out_ref.at[:, pl.ds(pl.multiple_of(uly * WIDTH, WIDTH), WIDTH)],
-            send_sem=out_send.at[u], recv_sem=out_recv.at[uly],
+    def out_copy(i, u):
+        return pltpu.make_async_remote_copy(
+            src_ref=done.at[i], dst_ref=out_ref.at[:, pl.ds(pl.multiple_of(uly * WIDTH, WIDTH), WIDTH)],
+            send_sem=out_send.at[i], recv_sem=out_recv.at[uly],
             device_id={"uly": u}, device_id_type=MESH,
         )
 
-    def out_keep(u):
+    def out_keep(i):
         return pltpu.make_async_copy(
-            done.at[u], out_ref.at[:, pl.ds(pl.multiple_of(uly * WIDTH, WIDTH), WIDTH)], out_local
+            done.at[i], out_ref.at[:, pl.ds(pl.multiple_of(uly * WIDTH, WIDTH), WIDTH)], out_local
         )
 
     for t in (0, 2, 1, 3):
@@ -430,33 +454,36 @@
             for j in range(2):
                 done[2 * t + j, :, h * DH : (h + 1) * DH] = flat[j * half : (j + 1) * half]
         for j in range(2):
-            u = 2 * t + j
+            u = 2 * turned(t) + j
 
             @pl.when(uly != u)
             def _():
-                out_copy(u).start()
+                out_copy(2 * t + j, u).start()
 
             @pl.when(uly == u)
             def _():
-                out_keep(u).start()
+                out_keep(2 * t + j).start()
 
     out_keep(0).wait()
-    for u in range(ulys):
+    for i in range(ulys):
+        u = 2 * turned(i // 2) + i % 2
 
         @pl.when(uly != u)
         def _():
+            out_copy(i, u).wait_send()
             pltpu.make_async_remote_copy(
-                src_ref=done.at[u], dst_ref=out_ref.at[:, u * WIDTH : (u + 1) * WIDTH],
-                send_sem=out_send.at[u], recv_sem=out_recv.at[u],
+                src_ref=done.at[i], dst_ref=out_ref.at[:, pl.ds(pl.multiple_of(u * WIDTH, WIDTH), WIDTH)],
+                send_sem=out_send.at[i], recv_sem=out_recv.at[u],
                 device_id={"uly": u}, device_id_type=MESH,
-            ).wait()
+            ).wait_recv()
 
     for slot, t in order:
         sib_copy(slot, t).wait_send()
     for t in range(tiles):
         far_copy(t).wait_send()
-        near_copy(0, t).wait_send()
-        near_copy(1, t).wait_send()
+        if (0, 2, 1, 3).index(t) >= tiles - DEPTH:
+            near_copy(0, t).wait_send()
+            near_copy(1, t).wait_send()
 
 
 def join(part, rows, zs, ulys):
@@ -482,7 +509,7 @@
             dma((ulys,)), dma((ulys,)), dma,
         ],
         compiler_params=pltpu.CompilerParams(
-            collective_id=1, has_side_effects=True, vmem_limit_bytes=48 * 1024 * 1024
+            collective_id=1, has_side_effects=True, vmem_limit_bytes=VMEM_LIMIT
         ),
         cost_estimate=pl.CostEstimate(flops=2 * 10**7, bytes_accessed=10**7, transcendentals=10**5),
     )(part)

time: 126 us -> 123 us (0.976)
  local copies, waits for them, and re-layouts: 7.81 us -> 2.06 us
  Pallas kernels: 118 us -> 120 us
    unnamed x13 -> x1, local copies, waits for them, and re-layouts: 7.81 us -> 2.06 us
    pallas_call x1, Pallas kernels: 32.1 us -> 36.9 us  [attend(): pl.pallas_call(attend_kernel, out_shape=jax.ShapeDtypeStruct((steps, PIEC...]
    pallas_call x1, Pallas kernels: 45.2 us -> 42.7 us  [join(): pl.pallas_call(functools.partial(join_kernel, zs), out_shape=jax.ShapeDty...]
where the time goes in v4:
time: 123 us; the launch traced here: 122 us
  Pallas kernels  120 us (98%)
  local copies, waits for them, and re-layouts  2.06 us (2%)
    pallas_call x1, Pallas kernels, join(): pl.pallas_call(functools.partial(join_kernel, zs), out_shape=jax.ShapeDty...  42.7 us
    pallas_call x1, Pallas kernels, spread(): pl.pallas_call(functools.partial(spread_kernel, zs), out_shape=(jax.Shape...  40.6 us
    pallas_call x1, Pallas kernels, attend(): pl.pallas_call(attend_kernel, out_shape=jax.ShapeDtypeStruct((steps, PIEC...  36.9 us

profile of v4, /device:TPU:24, one launch (start us, length us, event | category | flops | bytes accessed | tf_op | source)
XLA Modules:
  0.0 122.3 jit_solution(80634434430854663)
XLA Ops:
  0.0 40.6 %shard_map.64 = (bf16[4096,768]{1,0:T(8,128)(2,1)}, bf16[512,768]{1,0:T(8,128)(2,1)}, bf16[512,768]{1,0:T(8,128)(2,1)}) custom-call(bf16[64,6144]{1,0:T(8,128)(2,1)} %nq_ref.1, bf16[64,6144]{1,0:T(8,128)(2,1)} %nk_ref.1, bf16[64,6144]{1,0:T(8,128)(2,1)} %nv_ref.1), custom_call_target="tpu_custom_call" | custom-call | bytes 20000000 | tf_op jit(solution)/shard_map/pallas_call | solution.py:306
  40.7 36.9 %shard_map.65.part_ref = bf16[32,784,128]{2,1,0:T(8,128)(2,1)} custom-call(s32[1]{0:T(128)} %bitcast.blk_ref, s32[32,96]{1,0:T(8,128)} %flags_ref.1, bf16[4096,768]{1,0:T(8,128)(2,1)} %get-tuple-element.8.q_ref, bf16[1024,768]{1,0:T(8,128)(2,1)} %ck_ref.1, bf16[512,768]{1,0:T(8,128)(2,1)} %get-tuple-element.9.sk_ref, bf16[1024,768]{1,0:T(8,128)(2,1)} %cv_ref.1, ...), custom_call_target="tpu_custom_call" | custom-call | flops 6000000000 | bytes 18000000 | tf_op jit(solution)/shard_map/pallas_call | solution.py:135
  77.5 42.7 %shard_map.66 = bf16[64,6144]{1,0:T(8,128)(2,1)} custom-call(bf16[32,784,128]{2,1,0:T(8,128)(2,1)} %shard_map.65.part_ref), custom_call_target="tpu_custom_call" | custom-call | flops 20000000 | bytes 10000000 | tf_op jit(solution)/shard_map/pallas_call | solution.py:493
  120.3 2.1 %copy.8 = bf16[64,6144]{1,0:T(8,128)(2,1)} copy(bf16[64,6144]{1,0:T(8,128)(2,1)} %shard_map.66) | data formatting | bytes 1572864

commit v5 on v4

--- a/solution.py
+++ b/solution.py
@@ -16,6 +16,7 @@
 GROUP = 4
 PER = 4
 VMEM_LIMIT = 62 * 1024 * 1024
+FLIGHT = 7
 DEPTH = 1
 LOW = -1e30
 LOG2 = 1.4426950408889634 * DH ** (-0.5)
@@ -155,6 +156,9 @@
     )(blk, flags, queries, context_keys, span_keys, context_values, span_values)
 
 
+SHIFTS = ((0, 0), (1, 0), (0, 1), (0, 3), (1, 1), (1, 3), (0, 2), (1, 2))
+
+
 def spread_kernel(
     zs, nq_ref, nk_ref, nv_ref, q_ref, k_ref, v_ref, stage,
     keep_sem, q_send, q_recv, kv_send, kv_recv, own_send, ring_recv, pass_send, far_recv, sib_send, sib_recv,
@@ -180,19 +184,23 @@
     def span_rows(u):
         return pl.ds(pl.multiple_of(u * height, height), height)
 
+    def partner(d, sign):
+        across, along = SHIFTS[d]
+        return lax.rem(uly // 4 + across, 2) * 4 + lax.rem(uly + 4 + sign * along, 4)
+
     def q_rows(chip, side, d):
-        source = lax.rem(uly + ulys - d, ulys)
+        source = partner(d, -1)
         return pl.ds(pl.multiple_of(((chip * 2 + side) * ulys + source) * height, height), height)
 
     def q_copy(d):
-        target = lax.rem(uly + d, ulys)
+        target = partner(d, 1)
         return pltpu.make_async_remote_copy(
             src_ref=nq_ref.at[:, columns(target)], dst_ref=q_ref.at[q_rows(z, core, 0), :],
             send_sem=q_send.at[d], recv_sem=q_recv.at[d], device_id={"uly": target}, device_id_type=MESH,
         )
 
     def kv_copy(which, d):
-        target = lax.rem(uly + d, ulys)
+        target = partner(d, 1)
         src, dst = ((nk_ref, k_ref), (nv_ref, v_ref))[which]
         return pltpu.make_async_remote_copy(
             src_ref=src.at[:, columns(target)], dst_ref=dst.at[span_rows(uly), :],
@@ -203,9 +211,9 @@
     def kv_wait(which, d):
         src, dst = ((nk_ref, k_ref), (nv_ref, v_ref))[which]
         return pltpu.make_async_remote_copy(
-            src_ref=src.at[:, columns(uly)], dst_ref=dst.at[span_rows(lax.rem(uly + ulys - d, ulys)), :],
+            src_ref=src.at[:, columns(uly)], dst_ref=dst.at[span_rows(partner(d, -1)), :],
             send_sem=kv_send.at[which, d], recv_sem=kv_recv.at[which, d],
-            device_id={"uly": lax.rem(uly + d, ulys)}, device_id_type=MESH,
+            device_id={"uly": partner(d, 1)}, device_id_type=MESH,
         )
 
     def move(rows, send, recv, device):
@@ -258,7 +266,7 @@
 
     own_piece(own_send.at[0, 0], ring_recv.at[0, 0], ahead).start()
     own_piece(own_send.at[1, 0], ring_recv.at[1, 0], behind).start()
-    for d in range(1, ulys):
+    for d in range(1, 1 + FLIGHT):
         q_copy(d).start()
     own_piece(sib_send.at[0, 0], sib_recv.at[0, 0], sibling).start()
     for keep in keeps:
@@ -266,6 +274,9 @@
 
     for d in range(1, ulys):
         move(q_rows(z, core, d), q_send.at[d], q_recv.at[d], sibling).wait_recv()
+        if d + FLIGHT < ulys:
+            q_copy(d).wait_send()
+            q_copy(d + FLIGHT).start()
         to_ring(0, d).start()
         to_ring(1, d).start()
         to_sibling(0, d).start()
@@ -283,7 +294,8 @@
         to_sibling(3, d).start()
 
     for d in range(1, ulys):
-        q_copy(d).wait_send()
+        if d + FLIGHT >= ulys:
+            q_copy(d).wait_send()
         for which in range(2):
             kv_copy(which, d).wait_send()
             kv_wait(which, d).wait_recv()
@@ -509,7 +521,7 @@
             dma((ulys,)), dma((ulys,)), dma,
         ],
         compiler_params=pltpu.CompilerParams(
-            collective_id=1, has_side_effects=True, vmem_limit_bytes=VMEM_LIMIT
+            collective_id=1, has_side_effects=True, vmem_limit_bytes=48 * 1024 * 1024
         ),
         cost_estimate=pl.CostEstimate(flops=2 * 10**7, bytes_accessed=10**7, transcendentals=10**5),
     )(part)

time: 123 us -> 117 us (0.951)
  Pallas kernels: 120 us -> 115 us
    pallas_call x1, Pallas kernels: 40.6 us -> 37.5 us  [spread(): pl.pallas_call(functools.partial(spread_kernel, zs), out_shape=(jax.Shape...]
    pallas_call x1, Pallas kernels: 36.9 us -> 34.9 us  [attend(): pl.pallas_call(attend_kernel, out_shape=jax.ShapeDtypeStruct((steps, PIEC...]
where the time goes in v5:
time: 117 us; the launch traced here: 116 us
  Pallas kernels  115 us (98%)
    pallas_call x1, Pallas kernels, join(): pl.pallas_call(functools.partial(join_kernel, zs), out_shape=jax.ShapeDty...  42.4 us
    pallas_call x1, Pallas kernels, spread(): pl.pallas_call(functools.partial(spread_kernel, zs), out_shape=(jax.Shape...  37.5 us
    pallas_call x1, Pallas kernels, attend(): pl.pallas_call(attend_kernel, out_shape=jax.ShapeDtypeStruct((steps, PIEC...  34.9 us

profile of v5, /device:TPU:24, one launch (start us, length us, event | category | flops | bytes accessed | tf_op | source)
XLA Modules:
  0.0 115.7 jit_solution(16724439672422530027)
XLA Ops:
  0.0 37.5 %shard_map.64 = (bf16[4096,768]{1,0:T(8,128)(2,1)}, bf16[512,768]{1,0:T(8,128)(2,1)}, bf16[512,768]{1,0:T(8,128)(2,1)}) custom-call(bf16[64,6144]{1,0:T(8,128)(2,1)} %nq_ref.1, bf16[64,6144]{1,0:T(8,128)(2,1)} %nk_ref.1, bf16[64,6144]{1,0:T(8,128)(2,1)} %nv_ref.1), custom_call_target="tpu_custom_call" | custom-call | bytes 20000000 | tf_op jit(solution)/shard_map/pallas_call | solution.py:318
  37.5 34.9 %shard_map.65.part_ref = bf16[32,784,128]{2,1,0:T(8,128)(2,1)} custom-call(s32[1]{0:T(128)} %bitcast.blk_ref, s32[32,96]{1,0:T(8,128)} %flags_ref.1, bf16[4096,768]{1,0:T(8,128)(2,1)} %get-tuple-element.8.q_ref, bf16[1024,768]{1,0:T(8,128)(2,1)} %ck_ref.1, bf16[512,768]{1,0:T(8,128)(2,1)} %get-tuple-element.9.sk_ref, bf16[1024,768]{1,0:T(8,128)(2,1)} %cv_ref.1, ...), custom_call_target="tpu_custom_call" | custom-call | flops 6000000000 | bytes 18000000 | tf_op jit(solution)/shard_map/pallas_call | solution.py:136
  72.4 42.4 %shard_map.66 = bf16[64,6144]{1,0:T(8,128)(2,1)S(1)} custom-call(bf16[32,784,128]{2,1,0:T(8,128)(2,1)} %shard_map.65.part_ref), custom_call_target="tpu_custom_call" | custom-call | flops 20000000 | bytes 10000000 | tf_op jit(solution)/shard_map/pallas_call | solution.py:505
  114.8 0.9 copy.8

commit v6 on v5

--- a/solution.py
+++ b/solution.py
@@ -13,8 +13,9 @@
 WIDTH = HEADS * DH
 ROWS = 144
 PIECE = WIDTH + 16
-GROUP = 4
-PER = 4
+GROUP = 6
+STRIDE = 16
+LAG = 6
 VMEM_LIMIT = 62 * 1024 * 1024
 FLIGHT = 7
 DEPTH = 1
@@ -29,103 +30,171 @@
 
 
 def attend_kernel(
-    blk_ref, flags_ref, q_ref, ck_ref, sk_ref, cv_ref, sv_ref, o_ref, k_ref, v_ref, vt, acc, top, order_ref, sems
+    blk_ref, flags_ref, q_ref, ck_ref, sk_ref, cv_ref, sv_ref, o_ref,
+    k_ref, v_ref, vt, acc, top, q_buf, o_buf, k_list, counts, ranked, places, sems, q_sems, o_sems,
 ):
-    step = pl.program_id(0)
-    tiles = vt.shape[0]
+    q_tiles = o_ref.shape[0]
+    empty = vt.shape[0] - 1
+    tiles = empty
     ctx_rows = ck_ref.shape[0]
     ctx_tiles = ctx_rows // TILE
     span_tiles = tiles - ctx_tiles
     blk = blk_ref[0]
     first_span = flags_ref.shape[1] - flags_ref.shape[0]
-
-    @pl.when(step == 0)
-    def _():
-        copies = [
-            pltpu.make_async_copy(cv_ref, v_ref.at[:ctx_rows], sems.at[0]),
-            pltpu.make_async_copy(sv_ref, v_ref.at[ctx_rows:], sems.at[1]),
-            pltpu.make_async_copy(ck_ref, k_ref.at[:ctx_rows], sems.at[2]),
-            pltpu.make_async_copy(sk_ref, k_ref.at[ctx_rows:], sems.at[3]),
+    pairs = q_tiles // 2
+
+    copies = [
+        pltpu.make_async_copy(cv_ref, v_ref.at[:ctx_rows], sems.at[0]),
+        pltpu.make_async_copy(sv_ref, v_ref.at[ctx_rows:], sems.at[1]),
+        pltpu.make_async_copy(ck_ref, k_ref.at[:ctx_rows], sems.at[2]),
+        pltpu.make_async_copy(sk_ref, k_ref.at[ctx_rows:], sems.at[3]),
+    ]
+    for copy in copies:
+        copy.start()
+
+    for c in range(tiles + 1):
+        places[c] = 0
+
+    def gather(step, carry):
+        near = [2 * step, 2 * step + 1]
+        flags = [
+            [flags_ref[tile, blk * ctx_tiles + t] for t in range(ctx_tiles)]
+            + [flags_ref[tile, first_span + blk * span_tiles + t] for t in range(span_tiles)]
+            for tile in near
         ]
-        for copy in copies:
-            copy.start()
-        copies[0].wait()
-        copies[1].wait()
-
-        def turn(t, carry):
-            rows = pl.ds(pl.multiple_of(t * TILE, TILE), TILE)
-            for h in range(HEADS):
-                vt[t, h * ROWS : h * ROWS + DH, :] = v_ref[rows, h * DH : (h + 1) * DH].T
-                vt[t, h * ROWS + DH : (h + 1) * ROWS, :] = jnp.ones((ROWS - DH, TILE), jnp.bfloat16)
-            return carry
-
-        lax.fori_loop(0, tiles, turn, 0)
-        top[...] = jnp.full_like(top, LOW)
-        copies[2].wait()
-        copies[3].wait()
-
-    def one(sub, carry):
-        tile = step * PER + sub
-        q_rows = pl.ds(pl.multiple_of(sub * TILE, TILE), TILE)
-        count = jnp.int32(0)
-        for t in range(tiles):
-            column = blk * ctx_tiles + t if t < ctx_tiles else first_span + blk * span_tiles + t - ctx_tiles
-            order_ref[count] = t
-            count = count + jnp.where(flags_ref[tile, column] > 0, 1, 0)
-
-        def scores(h, picked):
+        for tile, row in zip(near, flags):
+            base = tile * STRIDE
+            count = jnp.int32(0)
+            for t in range(tiles):
+                k_list[base + count] = t
+                count = count + row[t]
+            counts[tile] = count
+            places[count] = places[count] + 1
+        return carry
+
+    lax.fori_loop(0, pairs, gather, 0)
+    run = jnp.int32(0)
+    for c in range(tiles, -1, -1):
+        held = places[c]
+        places[c] = run
+        run = run + held
+
+    def rank(tile, carry):
+        count = counts[tile]
+        place = places[count]
+        ranked[place] = tile
+        places[count] = place + 1
+        return carry
+
+    lax.fori_loop(0, q_tiles, rank, 0)
+
+    def q_copy(pair, slot, i):
+        tile = ranked[2 * pair + i]
+        rows = pl.ds(pl.multiple_of(tile * TILE, TILE), TILE)
+        return pltpu.make_async_copy(q_ref.at[rows, :], q_buf.at[slot, i], q_sems.at[slot, i])
+
+    def o_copy(tile, slot, i):
+        return pltpu.make_async_copy(o_buf.at[slot, i], o_ref.at[tile], o_sems.at[slot, i])
+
+    for i in range(2):
+        q_copy(0, 0, i).start()
+    copies[0].wait()
+    copies[1].wait()
+
+    def turn(t, carry):
+        rows = pl.ds(pl.multiple_of(t * TILE, TILE), TILE)
+        for h in range(HEADS):
+            vt[t, h * ROWS : h * ROWS + DH, :] = v_ref[rows, h * DH : (h + 1) * DH].T
+            vt[t, h * ROWS + DH : (h + 1) * ROWS, :] = jnp.ones((ROWS - DH, TILE), jnp.bfloat16)
+        return carry
+
+    lax.fori_loop(0, tiles, turn, 0)
+    vt[empty] = jnp.zeros(vt.shape[1:], vt.dtype)
+    top[...] = jnp.full_like(top, LOW)
+    copies[2].wait()
+    copies[3].wait()
+
+    def one(pair, carry):
+        slot = lax.rem(pair, 2)
+
+        @pl.when(pair + 1 < pairs)
+        def _():
+            for i in range(2):
+                q_copy(pair + 1, 1 - slot, i).start()
+
+        both = [ranked[2 * pair], ranked[2 * pair + 1]]
+        kept = [counts[tile] for tile in both]
+        n = jnp.maximum(kept[0], 1)
+        for i in range(2):
+            q_copy(pair, slot, i).wait()
+
+        def scores(i, h, ks):
             cols = slice(h * DH, (h + 1) * DH)
-            ks = [k_ref[pl.ds(pl.multiple_of(t * TILE, TILE), TILE), cols] for t in picked]
             return lax.dot_general(
-                jnp.concatenate(ks, axis=0),
-                q_ref[q_rows, cols],
+                jnp.concatenate([k_ref[pl.ds(pl.multiple_of(t * TILE, TILE), TILE), cols] for t in ks], axis=0),
+                q_buf[slot, i, :, cols],
                 (((1,), (1,)), ((), ())),
                 preferred_element_type=jnp.float32,
             )
 
-        def weigh(h, picked, s, first):
+        def weigh(i, h, vs, s, first):
             new = jnp.max(s, axis=0, keepdims=True)
             if not first:
-                old = top[h : h + 1, :]
+                old = top[i, h : h + 1, :]
                 new = jnp.maximum(old, new)
                 scale = jnp.exp2((old - new) * LOG2)
-            top[h : h + 1, :] = new
+            top[i, h : h + 1, :] = new
             p = jnp.exp2((s - new) * LOG2).astype(jnp.bfloat16)
-            vs = jnp.concatenate([vt[t, h * ROWS : (h + 1) * ROWS, :] for t in picked], axis=1)
-            got = jnp.dot(vs, p, preferred_element_type=jnp.float32)
-            acc[h] = got if first else acc[h] * scale + got
-
-        def visit(picked, first):
-            all_scores = [scores(h, picked) for h in range(HEADS)]
+            values = jnp.concatenate([vt[t, h * ROWS : (h + 1) * ROWS, :] for t in vs], axis=1)
+            got = jnp.dot(values, p, preferred_element_type=jnp.float32)
+            acc[i, h] = got if first else acc[i, h] * scale + got
+
+        def visit(at, width, first):
+            ks = [
+                [k_list[tile * STRIDE + jnp.minimum(at + a, jnp.maximum(count - 1, 0))] for a in range(width)]
+                for tile, count in zip(both, kept)
+            ]
+            vs = [
+                [jnp.where(at + a < count, ks[i][a], empty) for a in range(width)] for i, count in enumerate(kept)
+            ]
+            work = [(i, h) for i in range(2) for h in range(HEADS)]
+            found = [scores(i, h, ks[i]) for i, h in work[:LAG]]
+            for j, (i, h) in enumerate(work):
+                if j + LAG < len(work):
+                    i2, h2 = work[j + LAG]
+                    found.append(scores(i2, h2, ks[i2]))
+                weigh(i, h, vs[i], found[j], first)
+
+        lead = lax.rem(n + GROUP - 1, GROUP) + 1
+        lax.switch(lead - 1, [functools.partial(visit, 0, w, True) for w in range(1, GROUP + 1)])
+
+        def more(j, inner):
+            visit(lead + GROUP * j, GROUP, False)
+            return inner
+
+        lax.fori_loop(0, (n - lead) // GROUP, more, 0)
+
+        @pl.when(pair >= 2)
+        def _():
+            for i in range(2):
+                o_copy(0, slot, i).wait()
+
+        for i in range(2):
+            totals = [acc[i, h, DH : DH + 1, :] for h in range(HEADS)]
             for h in range(HEADS):
-                weigh(h, picked, all_scores[h], first)
-
-        def none():
-            acc[...] = jnp.zeros_like(acc)
-
-        def lead_visit(n):
-            visit([order_ref[a] for a in range(n)], True)
-
-        lead = jnp.where(count == 0, 0, lax.rem(count + GROUP - 1, GROUP) + 1)
-        lax.switch(lead, [none] + [functools.partial(lead_visit, n) for n in range(1, GROUP + 1)])
-
-        def more(j, inner):
-            visit([order_ref[lead + GROUP * j + a] for a in range(GROUP)], False)
-            return inner
-
-        lax.fori_loop(0, (count - lead) // GROUP, more, 0)
-
-        totals = [acc[h, DH : DH + 1, :] for h in range(HEADS)]
-        for h in range(HEADS):
-            safe = jnp.where(totals[h] > 0, totals[h], 1.0)
-            o_ref[sub, h * DH : (h + 1) * DH, :] = (acc[h, :DH, :] * (1.0 / safe)).astype(jnp.bfloat16)
-        total = jnp.concatenate(totals + [jnp.zeros((8 - HEADS, TILE), jnp.float32)], axis=0)
-        found = total > 0
-        lse = jnp.where(found, top[...] * LOG2 + jnp.log2(jnp.where(found, total, 1.0)), LOW)
-        o_ref[sub, WIDTH:PIECE, :] = split_low(lse)
+                safe = jnp.where(totals[h] > 0, totals[h], 1.0)
+                o_buf[slot, i, h * DH : (h + 1) * DH, :] = (acc[i, h, :DH, :] * (1.0 / safe)).astype(jnp.bfloat16)
+            total = jnp.concatenate(totals + [jnp.zeros((8 - HEADS, TILE), jnp.float32)], axis=0)
+            seen = total > 0
+            lse = jnp.where(seen, top[i] * LOG2 + jnp.log2(jnp.where(seen, total, 1.0)), LOW)
+            o_buf[slot, i, WIDTH:PIECE, :] = split_low(lse)
+            o_copy(both[i], slot, i).start()
         return carry
 
-    lax.fori_loop(0, PER, one, 0)
+    lax.fori_loop(0, pairs, one, 0)
+    for slot in range(2):
+        for i in range(2):
+            o_copy(0, slot, i).wait()
 
 
 def attend(blk, flags, queries, context_keys, span_keys, context_values, span_values):
@@ -133,22 +202,30 @@
     rows = context_keys.shape[0] + span_keys.shape[0]
     tiles = rows // TILE
     anywhere = pl.BlockSpec(memory_space=pl.ANY)
+    number = pltpu.SMEM
     return pl.pallas_call(
         attend_kernel,
         out_shape=jax.ShapeDtypeStruct((steps, PIECE, TILE), jnp.bfloat16),
         grid_spec=pltpu.PrefetchScalarGridSpec(
             num_scalar_prefetch=2,
-            grid=(steps // PER,),
-            in_specs=[pl.BlockSpec((TILE * PER, WIDTH), lambda i, *_: (i, 0))] + [anywhere] * 4,
-            out_specs=pl.BlockSpec((PER, PIECE, TILE), lambda i, *_: (i, 0, 0)),
+            grid=(1,),
+            in_specs=[anywhere] * 5,
+            out_specs=anywhere,
             scratch_shapes=[
                 pltpu.VMEM((rows, WIDTH), jnp.bfloat16),
                 pltpu.VMEM((rows, WIDTH), jnp.bfloat16),
-                pltpu.VMEM((tiles, HEADS * ROWS, TILE), jnp.bfloat16),
-                pltpu.VMEM((HEADS, ROWS, TILE), jnp.float32),
-                pltpu.VMEM((8, TILE), jnp.float32),
-                pltpu.SMEM((tiles,), jnp.int32),
+                pltpu.VMEM((tiles + 1, HEADS * ROWS, TILE), jnp.bfloat16),
+                pltpu.VMEM((2, HEADS, ROWS, TILE), jnp.float32),
+                pltpu.VMEM((2, 8, TILE), jnp.float32),
+                pltpu.VMEM((2, 2, TILE, WIDTH), jnp.bfloat16),
+                pltpu.VMEM((2, 2, PIECE, TILE), jnp.bfloat16),
+                number((steps * STRIDE,), jnp.int32),
+                number((steps,), jnp.int32),
+                number((steps,), jnp.int32),
+                number((tiles + 1,), jnp.int32),
                 pltpu.SemaphoreType.DMA((4,)),
+                pltpu.SemaphoreType.DMA((2, 2)),
+                pltpu.SemaphoreType.DMA((2, 2)),
             ],
         ),
         compiler_params=pltpu.CompilerParams(vmem_limit_bytes=VMEM_LIMIT),

time: 117 us -> 114 us (0.974)
  Pallas kernels: 115 us -> 111 us
    pallas_call x1, Pallas kernels: 34.9 us -> 31 us  [attend(): pl.pallas_call(attend_kernel, out_shape=jax.ShapeDtypeStruct((steps, PIEC...]
where the time goes in v6:
time: 114 us; the launch traced here: 112 us
  Pallas kernels  111 us (97%)
    pallas_call x1, Pallas kernels, join(): pl.pallas_call(functools.partial(join_kernel, zs), out_shape=jax.ShapeDty...  42.8 us
    pallas_call x1, Pallas kernels, spread(): pl.pallas_call(functools.partial(spread_kernel, zs), out_shape=(jax.Shape...  37.5 us
    pallas_call x1, Pallas kernels, attend(): pl.pallas_call(attend_kernel, out_shape=jax.ShapeDtypeStruct((steps, PIEC...  31 us

profile of v6, /device:TPU:24, one launch (start us, length us, event | category | flops | bytes accessed | tf_op | source)
XLA Modules:
  0.0 112.2 jit_solution(12659443455483786463)
XLA Ops:
  0.0 37.5 %shard_map.64 = (bf16[4096,768]{1,0:T(8,128)(2,1)}, bf16[512,768]{1,0:T(8,128)(2,1)}, bf16[512,768]{1,0:T(8,128)(2,1)}) custom-call(bf16[64,6144]{1,0:T(8,128)(2,1)} %nq_ref.1, bf16[64,6144]{1,0:T(8,128)(2,1)} %nk_ref.1, bf16[64,6144]{1,0:T(8,128)(2,1)} %nv_ref.1), custom_call_target="tpu_custom_call" | custom-call | bytes 20000000 | tf_op jit(solution)/shard_map/pallas_call | solution.py:395
  37.5 31.0 %shard_map.65.part_ref = bf16[32,784,128]{2,1,0:T(8,128)(2,1)} custom-call(s32[1]{0:T(128)} %bitcast.blk_ref, s32[32,96]{1,0:T(8,128)} %flags_ref.1, bf16[4096,768]{1,0:T(8,128)(2,1)} %get-tuple-element.8.q_ref, bf16[1024,768]{1,0:T(8,128)(2,1)} %ck_ref.1, bf16[512,768]{1,0:T(8,128)(2,1)} %get-tuple-element.9.sk_ref, bf16[1024,768]{1,0:T(8,128)(2,1)} %cv_ref.1, ...), custom_call_target="tpu_custom_call" | custom-call | flops 6000000000 | bytes 18000000 | tf_op jit(solution)/shard_map/pallas_call | solution.py:206
  68.5 42.8 %shard_map.66 = bf16[64,6144]{1,0:T(8,128)(2,1)S(1)} custom-call(bf16[32,784,128]{2,1,0:T(8,128)(2,1)} %shard_map.65.part_ref), custom_call_target="tpu_custom_call" | custom-call | flops 20000000 | bytes 10000000 | tf_op jit(solution)/shard_map/pallas_call | solution.py:582
  111.3 0.9 copy.8

commit v7 on v6

--- a/solution.py
+++ b/solution.py
@@ -13,9 +13,9 @@
 WIDTH = HEADS * DH
 ROWS = 144
 PIECE = WIDTH + 16
-GROUP = 6
+GROUP = 4
 STRIDE = 16
-LAG = 6
+LAG = 5
 VMEM_LIMIT = 62 * 1024 * 1024
 FLIGHT = 7
 DEPTH = 1

time: 114 us -> 111 us (0.974)
  Pallas kernels: 111 us -> 109 us
    pallas_call x1, Pallas kernels: 31 us -> 26.9 us  [attend(): pl.pallas_call(attend_kernel, out_shape=jax.ShapeDtypeStruct((steps, PIEC...]
    pallas_call x1, Pallas kernels: 42.8 us -> 45 us  [join(): pl.pallas_call(functools.partial(join_kernel, zs), out_shape=jax.ShapeDty...]
where the time goes in v7:
time: 111 us; the launch traced here: 110 us
  Pallas kernels  109 us (98%)
    pallas_call x1, Pallas kernels, join(): pl.pallas_call(functools.partial(join_kernel, zs), out_shape=jax.ShapeDty...  45 us
    pallas_call x1, Pallas kernels, spread(): pl.pallas_call(functools.partial(spread_kernel, zs), out_shape=(jax.Shape...  37.5 us
    pallas_call x1, Pallas kernels, attend(): pl.pallas_call(attend_kernel, out_shape=jax.ShapeDtypeStruct((steps, PIEC...  26.9 us

profile of v7, /device:TPU:24, one launch (start us, length us, event | category | flops | bytes accessed | tf_op | source)
XLA Modules:
  0.0 110.3 jit_solution(14667419081005686514)
XLA Ops:
  0.0 37.5 %shard_map.64 = (bf16[4096,768]{1,0:T(8,128)(2,1)}, bf16[512,768]{1,0:T(8,128)(2,1)}, bf16[512,768]{1,0:T(8,128)(2,1)}) custom-call(bf16[64,6144]{1,0:T(8,128)(2,1)} %nq_ref.1, bf16[64,6144]{1,0:T(8,128)(2,1)} %nk_ref.1, bf16[64,6144]{1,0:T(8,128)(2,1)} %nv_ref.1), custom_call_target="tpu_custom_call" | custom-call | bytes 20000000 | tf_op jit(solution)/shard_map/pallas_call | solution.py:395
  37.5 26.9 %shard_map.65.part_ref = bf16[32,784,128]{2,1,0:T(8,128)(2,1)} custom-call(s32[1]{0:T(128)} %bitcast.blk_ref, s32[32,96]{1,0:T(8,128)} %flags_ref.1, bf16[4096,768]{1,0:T(8,128)(2,1)} %get-tuple-element.8.q_ref, bf16[1024,768]{1,0:T(8,128)(2,1)} %ck_ref.1, bf16[512,768]{1,0:T(8,128)(2,1)} %get-tuple-element.9.sk_ref, bf16[1024,768]{1,0:T(8,128)(2,1)} %cv_ref.1, ...), custom_call_target="tpu_custom_call" | custom-call | flops 6000000000 | bytes 18000000 | tf_op jit(solution)/shard_map/pallas_call | solution.py:206
  64.4 45.0 %shard_map.66 = bf16[64,6144]{1,0:T(8,128)(2,1)S(1)} custom-call(bf16[32,784,128]{2,1,0:T(8,128)(2,1)} %shard_map.65.part_ref), custom_call_target="tpu_custom_call" | custom-call | flops 20000000 | bytes 10000000 | tf_op jit(solution)/shard_map/pallas_call | solution.py:582
  109.5 0.9 copy.8
